TPU v7x, 32 devices: a whole 2x2x4 slice. The times are simulated.
32 devices in a mesh: tm: 8 (over z, y), chan: 4 (over x, core).
Axes of the slice: x: 2, y: 2, z: 4, core: 2. Of those that a mesh axis runs over, the one named last changes fastest.
Arguments:
- spectrogram_input: bfloat16 [512, 8192], P('chan', 'tm'), may hold values from -6 to 6
- upsample_direction: float32 [16, 256, 512], P(None, 'chan'), may hold values from -0.09375 to 0.09375
- upsample_magnitude: float32 [512], replicated, may hold values from 0.5 to 2
- upsample_bias: float32 [256], P('chan'), may hold values from -3 to 3
- dilated_direction: float32 [3, 3, 256, 256], P(None, None, 'chan'), may hold values from -0.21875 to 0.21875
- dilated_magnitude: float32 [3, 256], P(None, 'chan'), may hold values from 0.5 to 2
- dilated_bias: float32 [3, 256], P(None, 'chan'), may hold values from -3 to 3
- pointwise_direction: float32 [3, 256, 256], P(None, 'chan'), may hold values from -0.375 to 0.375
- pointwise_magnitude: float32 [3, 256], P(None, 'chan'), may hold values from 0.5 to 2
- block_output_bias: float32 [3, 256], P(None, 'chan'), may hold values from -3 to 3
- shortcut_direction: float32 [3, 256, 256], P(None, 'chan'), may hold values from -0.375 to 0.375
- shortcut_magnitude: float32 [3, 256], P(None, 'chan'), may hold values from 0.5 to 2
- cotangent: bfloat16 [256, 65536], P('chan', 'tm'), may hold values from -6 to 6
- silence: int32 [65536], P('tm'), may hold values 0 or 1
- segments: int32 [8192], replicated, may hold values from 0 to 4, as said below
Outputs:
- activation: bfloat16 [256, 65536], P('chan', 'tm')
- input_grad: bfloat16 [512, 8192], P('chan', 'tm')
- up_v_grad: float32 [16, 256, 512], P(None, 'chan')
- up_g_grad: float32 [512], replicated
- up_b_grad: float32 [256], P('chan')
- dilated_direction_gradient: float32 [3, 3, 256, 256], P(None, None, 'chan')
- dil_g_grad: float32 [3, 256], P(None, 'chan')
- dilated_bias_gradient: float32 [3, 256], P(None, 'chan')
- mix_v_grad: float32 [3, 256, 256], P(None, 'chan')
- mix_g_grad: float32 [3, 256], P(None, 'chan')
- out_b_grad: float32 [3, 256], P(None, 'chan')
- skip_v_grad: float32 [3, 256, 256], P(None, 'chan')
- skip_g_grad: float32 [3, 256], P(None, 'chan')
Inputs may be any that keep to these rules, and one draw needn't show every extreme that they name: `segments`: segment numbers of the frames never fall; they rise by one at each segment's first frame, and such rises occur only within the first 1024 and the last 1024 frames (never at frame 0, 1024 or 8192 - 1024).
All inputs are finite; a program needn't handle non-finite values. No bound on the sum of `silence` on one device may be relied on, other than what follows from the above.
Results may differ from a plain program's by a relative error of at most 0.028.
Values may be sent and summed in bfloat16 or wider, within the bound.
No kernel may reach another device: no remote copies, remote signals or barrier semaphores. Data moves between devices by JAX's collectives and lax.ppermute only.
A program may use at most 192 MiB of HBM per device.

v0:
```python
import functools

import jax
import jax.numpy as jnp
import numpy as np
from jax import lax
from jax.experimental import pallas as pl
from jax.experimental.pallas import tpu as pltpu
from jax.sharding import PartitionSpec as P

BF = jnp.bfloat16
F32 = jnp.float32
LANES = 128
HALO = 128
TAIL = 128
SUMS = 16
VMEM_LIMIT = 20 * 1024 * 1024


def swap(values, axis, bit):
    count = lax.axis_size(axis)
    return lax.ppermute(values, axis, [(k, k ^ bit) for k in range(count)])


def bits_of(count):
    bits = []
    bit = 1
    while bit < count:
        bits.append(bit)
        bit = 2 * bit
    return bits


def order_of(bits):
    order = [0]
    for bit in reversed(bits):
        order = order + [slot + bit for slot in order]
    return order


def gather_chan(own):
    held = {0: own}
    for bit in reversed(bits_of(lax.axis_size("chan"))):
        for slot in list(held):
            held[slot ^ bit] = swap(held[slot], "chan", bit)
    return [held[slot] for slot in range(len(held))]


def exchange_chan(pieces):
    return [pieces[0]] + [swap(pieces[s], "chan", s) for s in range(1, len(pieces))]


HBM = pl.BlockSpec(memory_space=pltpu.HBM)
VMEM = pl.BlockSpec(memory_space=pltpu.VMEM)


def kernel_call(body, outs, args, specs, scratch=(), micros=1.0):
    held = []
    in_specs = []
    operands = []
    for arg, spec in zip(args, specs, strict=True):
        in_specs.append({"H": HBM, "F": HBM, "R": VMEM, "V": VMEM}[spec])
        if spec == "F":
            held.append(pltpu.VMEM(arg.shape, arg.dtype))
        if spec == "R":
            arg = pltpu.with_memory_space_constraint(arg, pltpu.VMEM)
        if spec in "HF":
            arg = pltpu.with_memory_space_constraint(arg, pltpu.HBM)
        operands.append(arg)
    out_shape = []
    out_specs = []
    for shape, dtype, spec in outs:
        out_specs.append(HBM if spec == "H" else VMEM)
        spaced = {"R": pltpu.VMEM, "H": pltpu.HBM, "V": jax.ShapeDtypeStruct}[spec]
        out_shape.append(spaced(shape, dtype))
    fetched = len(held)

    def wrapped(*refs):
        refs = list(refs)
        if fetched:
            sems = refs.pop()
            targets = refs[-fetched:]
            refs = refs[:-fetched]
            sources = [number for number, spec in enumerate(specs) if spec == "F"]
            fetch([(refs[n], target) for n, target in zip(sources, targets)], sems)
            for n, target in zip(sources, targets):
                refs[n] = target
        body((lax.axis_index("tm"), lax.axis_index("chan")), *refs)

    extra = held + ([pltpu.SemaphoreType.DMA((fetched,))] if fetched else [])
    return pl.pallas_call(
        wrapped,
        out_shape=tuple(out_shape),
        in_specs=in_specs,
        out_specs=tuple(out_specs),
        scratch_shapes=list(scratch) + extra,
        compiler_params=pltpu.CompilerParams(vmem_limit_bytes=VMEM_LIMIT),
        cost_estimate=pl.CostEstimate(
            flops=int(micros * 1.1e9), bytes_accessed=0, transcendentals=0
        ),
    )(*operands)


def fetch(pairs, sems):
    copies = [
        pltpu.make_async_copy(source, target, sems.at[number])
        for number, (source, target) in enumerate(pairs)
    ]
    for copy in copies:
        copy.start()
    for copy in copies:
        copy.wait()


def unit(values):
    th = jnp.tanh(0.5 * values)
    base = 0.6 + 0.4 * th
    return values * base, base + 0.2 * values * (1.0 - th * th)


def unit_act(values):
    return values * (0.6 + 0.4 * jnp.tanh(0.5 * values))


def dot(left, right):
    return lax.dot_general(left, right, (((1,), (0,)), ((), ())), preferred_element_type=F32)


def dot_rt(left, right):
    return lax.dot_general(left, right, (((1,), (1,)), ((), ())), preferred_element_type=F32)


def eye_mask(count):
    rows = lax.broadcasted_iota(jnp.int32, (count, count), 0)
    cols = lax.broadcasted_iota(jnp.int32, (count, count), 1)
    return rows == cols


def to_col(row, eye):
    return jnp.sum(jnp.where(eye, row, 0.0), axis=1, keepdims=True)


def to_row(col, eye):
    return jnp.sum(jnp.where(eye, col, 0.0), axis=0, keepdims=True)


def at(start, size, step):
    return pl.ds(pl.multiple_of(start, step), size)


def edge_kernel(idx, spectrogram, cot, sil, ahead, behind, front, back, sound, mask, sems):
    rows = spectrogram.shape[0]
    frames, count = spectrogram.shape[1], cot.shape[1]
    low, high = pl.ds(0, HALO), pl.ds(count - HALO, HALO)
    fetch(
        [
            (spectrogram.at[:, frames - LANES :], front),
            (spectrogram.at[:, :LANES], back),
            (cot.at[:, high], sound.at[0]),
            (cot.at[:, low], sound.at[1]),
            (sil.at[:, high], mask.at[0]),
            (sil.at[:, low], mask.at[1]),
        ],
        sems,
    )
    ahead[0:rows, :] = front[...]
    behind[0:rows, :] = back[...]
    ahead[rows:, :] = (sound[0].astype(F32) * mask[0].astype(F32)).astype(BF)
    behind[rows:, :] = (sound[1].astype(F32) * mask[1].astype(F32)).astype(BF)


def square_kernel(idx, up_v, up_sq):
    total = jnp.zeros((up_v.shape[1], up_v.shape[2]), F32)
    for k in range(up_v.shape[0]):
        rows = up_v[k]
        total = total + rows * rows
    up_sq[...] = jnp.sum(total, axis=0, keepdims=True)


def prep_kernel(
    idx, dil_v, dil_g, dil_b, mix_v, mix_g, out_b, skip_v, skip_g, up_g, up_b, packed, near, far, up_row, bias_row
):
    up_row[...] = up_g[...]
    bias_row[...] = up_b[...]
    local_out = dil_v.shape[2]
    eye = eye_mask(local_out)
    lane = lax.broadcasted_iota(jnp.int32, (local_out, TAIL), 1)
    width = dil_v.shape[3]
    for j in range(dil_v.shape[0]):
        rows = pl.ds(j * local_out, local_out)
        square = jnp.zeros((local_out, 1), F32)
        for k in range(3):
            v = dil_v[j, k]
            square = square + jnp.sum(v * v, axis=1, keepdims=True)
        norm = jnp.sqrt(square)
        scale = to_col(dil_g[j : j + 1, :], eye) / norm
        for k in range(3):
            packed[rows, k * width : (k + 1) * width] = (dil_v[j, k] * scale).astype(BF)
        for number, (vref, gref) in enumerate(((mix_v, mix_g), (skip_v, skip_g))):
            v = vref[j]
            norm = jnp.sqrt(jnp.sum(v * v, axis=1, keepdims=True))
            scale = to_col(gref[j : j + 1, :], eye) / norm
            packed[rows, (3 + number) * width : (4 + number) * width] = (v * scale).astype(BF)
        first = to_col(dil_b[j : j + 1, :], eye)
        second = to_col(out_b[j : j + 1, :], eye)
        high_one = first.astype(BF).astype(F32)
        high_two = second.astype(BF).astype(F32)
        tail = jnp.where(lane == 0, high_one, 0.0) + jnp.where(lane == 1, first - high_one, 0.0)
        tail = tail + jnp.where(lane == 2, high_two, 0.0)
        tail = tail + jnp.where(lane == 3, second - high_two, 0.0)
        packed[rows, 5 * width : 5 * width + TAIL] = tail.astype(BF)
    half = near.shape[0]
    for number, target in enumerate((near, far)):
        target[...] = packed[at(((idx[0] ^ number) & 1) * half, half, 16), :]


def cut_kernel(pieces, idx, cot, sil, low, high, *refs):
    outs, wide = refs[:pieces], refs[pieces]
    count = cot.shape[1]
    own = count // pieces
    rows = cot.shape[0]
    wide[:, 0:HALO] = low[low.shape[0] - rows :, :]
    wide[:, HALO : HALO + count] = (cot[...].astype(F32) * sil[...].astype(F32)).astype(BF)
    wide[:, HALO + count :] = high[high.shape[0] - rows :, :]
    for s in range(pieces):
        outs[s][...] = wide[:, at((idx[1] ^ s) * own, own + 2 * HALO, LANES)]


def weight_kernel(pieces, blocks, idx, *refs):
    *parts, plain, dil_t, point_t = refs
    rows = parts[0].shape[0] // blocks
    part = rows // 2
    for s in range(pieces):
        start = (idx[1] ^ s) * rows
        if s < 2:
            for j in range(blocks):
                plain[j, at(start, rows, 16), :] = parts[s][j * rows : (j + 1) * rows, :]
            continue
        for number in range(2):
            source = parts[2 + 2 * (s - 2) + number]
            first = blocks * ((idx[0] ^ number) & 1)
            for q in range(blocks):
                place = first + q
                plain[
                    lax.div(place, 2), at(start + lax.rem(place, 2) * part, part, 16), :
                ] = source[q * part : (q + 1) * part, :]
    width = plain.shape[1]
    unit_matrix = jnp.where(eye_mask(width), 1.0, 0.0).astype(BF)
    for j in range(blocks):
        for k in range(5):
            turned = dot_rt(unit_matrix, plain[j, :, k * width : (k + 1) * width]).astype(BF)
            if k < 3:
                dil_t[j, :, k * width : (k + 1) * width] = turned
            else:
                point_t[j, :, (k - 3) * width : (k - 2) * width] = turned


def up_kernel(pieces, idx, *refs):
    mains, sides = refs[:pieces], refs[pieces : 2 * pieces]
    up_v, up_sq, up_g, up_b, frame_id, order = refs[2 * pieces : 2 * pieces + 6]
    outs = refs[2 * pieces + 6 : 3 * pieces + 6]
    act_hbm, up_hbm = refs[3 * pieces + 6 : 3 * pieces + 8]
    raw, stacked, phases, wide, act_out, up_w, held_v, held_order, *sems = refs[3 * pieces + 8 :]
    sems, out_sems = sems
    rows, frames = mains[0].shape
    local_out = up_v.shape[1]
    early = [
        pltpu.make_async_copy(up_v, held_v, sems.at[0]),
        pltpu.make_async_copy(order, held_order, sems.at[1]),
    ]
    for copy in early:
        copy.start()
    for s in range(pieces):
        here = at((idx[1] ^ s) * rows, rows, 16)
        raw[here, 0:LANES] = sides[s][:, 0:LANES]
        raw[here, LANES : LANES + frames] = mains[s][...]
        raw[here, LANES + frames :] = sides[s][:, LANES:]
    kept = [
        pltpu.make_async_copy(up_w, up_hbm, out_sems.at[0]),
        pltpu.make_async_copy(act_out, act_hbm, out_sems.at[1]),
    ]
    total = frames + 2 * LANES
    count = stacked.shape[1]
    channels = raw.shape[0]
    shift = total - (LANES - HALO // 8)
    ids = pltpu.roll(jnp.broadcast_to(frame_id[...], (8, total)), shift, axis=1)
    before = pltpu.roll(ids, 1, axis=1)
    after = pltpu.roll(ids, total - 1, axis=1)
    left = jnp.where(before == ids, 1.0, 0.0)[0:1, :].astype(BF)
    right = jnp.where(after == ids, 1.0, 0.0)[0:1, :].astype(BF)
    step = channels
    for r0 in range(0, channels, step):
        part = pl.ds(r0, step)
        acted = unit_act(raw[part, :].astype(F32)).astype(BF)
        act_out[part, :] = acted[:, LANES : LANES + frames]
        moved = pltpu.roll(acted, shift, axis=1)
        one = pltpu.roll(moved, 1, axis=1) * left
        two = pltpu.roll(moved, total - 1, axis=1) * right
        stacked[part, :] = moved[:, 0:count]
        stacked[pl.ds(channels + r0, step), :] = one[:, 0:count]
        stacked[pl.ds(2 * channels + r0, step), :] = two[:, 0:count]
    kept[1].start()
    early[0].wait()
    scale = up_g[...] / jnp.sqrt(up_sq[...])
    for k in range(up_v.shape[0]):
        up_w[k * local_out : (k + 1) * local_out, :] = (held_v[k] * scale).astype(BF)
    kept[0].start()
    eye = eye_mask(local_out)
    bias = to_col(up_b[...], eye)
    bias4 = jnp.concatenate([bias] * 4, axis=0)
    quarter = 4 * local_out
    for c0 in range(0, count, 3 * LANES):
        cols = pl.ds(c0, 3 * LANES)
        center = stacked[0:channels, cols]
        low = dot(up_w[quarter : 2 * quarter, :], center)
        low = low + dot(up_w[3 * quarter : 4 * quarter, :], stacked[channels : 2 * channels, cols])
        high = dot(up_w[2 * quarter : 3 * quarter, :], center)
        high = high + dot(up_w[0:quarter, :], stacked[2 * channels : 3 * channels, cols])
        low = (low + bias4).astype(BF)
        high = (high + bias4).astype(BF)
        for b in range(3):
            block = c0 // LANES + b
            if block * local_out >= phases.shape[0]:
                continue
            for r in range(8):
                source = (low, high)[r // 4]
                phases[block * local_out : (block + 1) * local_out, r * LANES : (r + 1) * LANES] = (
                    source[
                        (r % 4) * local_out : (r % 4 + 1) * local_out,
                        b * LANES : (b + 1) * LANES,
                    ]
                )
    early[1].wait()
    turned = dot(phases[...], held_order[...]).astype(BF)
    for block in range(count // LANES):
        wide[:, block * 1024 : (block + 1) * 1024] = turned[
            block * local_out : (block + 1) * local_out, :
        ]
    own = 8 * frames // pieces
    for s in range(pieces):
        outs[s][...] = wide[:, at((idx[1] ^ s) * own, own + 2 * HALO, LANES)]
    for copy in kept:
        copy.wait()


def sample_masks(sample_id, distance):
    width = sample_id.shape[1]
    ids = jnp.broadcast_to(sample_id[...], (8, width))
    back = pltpu.roll(ids, distance, axis=1)
    ahead = pltpu.roll(ids, width - distance, axis=1)
    return (
        jnp.where(back == ids, 1.0, 0.0)[0:1, :].astype(BF),
        jnp.where(ahead == ids, 1.0, 0.0)[0:1, :].astype(BF),
    )


def forward_kernel(pieces, blocks, idx, *refs):
    parts = refs[:pieces]
    plain, sample_id, silence = refs[pieces : pieces + 3]
    outs = refs[pieces + 3 : 2 * pieces + 3]
    kept = refs[2 * pieces + 3 : 2 * pieces + 8]
    hidden, taps, pair, final = refs[2 * pieces + 8 :]
    keep_h, keep_u, keep_m, keep_sh, keep_sc = kept
    rows, width = parts[0].shape
    channels = pieces * rows
    for s in range(pieces):
        hidden[at((idx[1] ^ s) * rows, rows, 16), :] = parts[s][...]
    for j in range(blocks):
        distance = 3**j
        tail = plain[j, :, 5 * channels : 5 * channels + TAIL].astype(F32)
        dil_b = tail[:, 0:1] + tail[:, 1:2]
        out_b = tail[:, 2:3] + tail[:, 3:4]

        low = hidden[...]
        keep_h[j] = low
        pair[channels : 2 * channels, :] = low
        acted, slope = unit(low.astype(F32))
        acted = acted.astype(BF)
        taps[channels : 2 * channels, :] = acted
        keep_u[j] = acted
        keep_sh[j] = slope.astype(BF)
        back, ahead = sample_masks(sample_id, distance)
        center = taps[channels : 2 * channels, :]
        taps[0:channels, :] = pltpu.roll(center, distance, axis=1) * back
        taps[2 * channels : 3 * channels, :] = pltpu.roll(center, width - distance, axis=1) * ahead

        inner = dot(plain[j, :, 0 : 3 * channels], taps[...]) + dil_b
        acted, slope = unit(inner)
        acted = acted.astype(BF)
        pair[0:channels, :] = acted
        keep_m[j] = acted
        keep_sc[j] = slope.astype(BF)
        after = dot(plain[j, :, 3 * channels : 5 * channels], pair[...]) + out_b
        if j < blocks - 1:
            hidden[...] = after.astype(BF)
        else:
            final[...] = after
    own = width - 2 * HALO
    voiced = silence[:, at(idx[1] * own, own, LANES)].astype(F32)
    for s in range(pieces):
        here = at((idx[1] ^ s) * rows, rows, 16)
        outs[s][...] = (final[here, HALO : HALO + own] * voiced).astype(BF)


def spread_taps(j, center, sample_id, taps):
    channels, width = center.shape
    distance = 3**j
    back, ahead = sample_masks(sample_id, distance)
    taps[channels : 2 * channels, :] = center
    taps[0:channels, :] = pltpu.roll(center, width - distance, axis=1) * ahead
    taps[2 * channels : 3 * channels, :] = pltpu.roll(center, distance, axis=1) * back


def edge_start(pieces, peer):
    return jnp.where(peer < pieces // 2, 0, HALO)


def backward_kernel(pieces, idx, *refs):
    parts = refs[:pieces]
    dil_t, point_t, sample_id, keep_sh, keep_sc = refs[pieces : pieces + 5]
    outs = refs[pieces + 5 : 2 * pieces + 5]
    errs, inners, taps, low = refs[2 * pieces + 5 :]
    rows = parts[0].shape[0]
    blocks, channels, width = errs.shape
    last = blocks - 1
    for s in range(pieces):
        errs[last, at((idx[1] ^ s) * rows, rows, 16), :] = parts[s][...]
    for j in reversed(range(blocks)):
        err = errs[j]
        inner = dot(point_t[j, :, 0:channels], err) * keep_sc[j].astype(F32)
        inner = inner.astype(BF)
        inners[j] = inner
        spread_taps(j, inner, sample_id, taps)
        spread = dot(dil_t[j], taps[...]) * keep_sh[j].astype(F32)
        after = (spread + dot(point_t[j, :, channels : 2 * channels], err)).astype(BF)
        if j > 0:
            errs[j - 1] = after
        else:
            low[...] = after
    lanes = at(edge_start(pieces, idx[1]), width - HALO, LANES)
    for s in range(pieces):
        outs[s][...] = low[at((idx[1] ^ s) * rows, rows, 16), lanes]


def grad_kernel(pieces, sequence, idx, errs, inners, sample_id, keep_h, keep_u, keep_m, *refs):
    keep, send, taps, mats = refs
    blocks, channels, width = errs.shape
    inside = pl.ds(HALO, width - 2 * HALO)
    rows = channels // pieces
    lane = lax.broadcasted_iota(jnp.int32, (channels, channels), 1)
    tail = jnp.zeros((channels, channels), F32)
    for j in range(blocks):
        spread_taps(j, inners[j], sample_id, taps)
        err = errs[j, :, inside]
        mats[5 * j + 3] = dot_rt(err, keep_m[j, :, inside]).astype(BF)
        mats[5 * j + 4] = dot_rt(err, keep_h[j, :, inside]).astype(BF)
        for k in range(3):
            mats[5 * j + k] = dot_rt(
                taps[k * channels : (k + 1) * channels, inside], keep_u[j, :, inside]
            ).astype(BF)
        dil_sum = jnp.sum(inners[j, :, inside].astype(F32), axis=1, keepdims=True)
        out_sum = jnp.sum(err.astype(F32), axis=1, keepdims=True)
        tail = tail + jnp.where(lane == 2 * j, dil_sum, 0.0)
        tail = tail + jnp.where(lane == 2 * j + 1, out_sum, 0.0)
    mats[5 * blocks] = tail.astype(BF)
    size = (5 * blocks + 1) * rows * pieces // len(sequence)
    part = min(size, rows)
    half = len(sequence) // 2
    for position, (s, t) in enumerate(sequence):
        target = (keep, send)[position // half]
        for q in range(size // part):
            place = (idx[0] ^ t) * (size // part) + q
            row = (idx[1] ^ s) * rows + lax.rem(place, rows // part) * part
            start = position % half * size + q * part
            target[start : start + part, :] = mats[
                lax.div(place, rows // part), at(row, part, 16), :
            ]


def halve_kernel(idx, keep, got, next_keep, next_send):
    half = next_keep.shape[0]
    total = keep[...].astype(F32) + got[...].astype(F32)
    next_keep[...] = total[:half].astype(BF)
    next_send[...] = total[half:].astype(BF)


def up_back_kernel(pieces, peers, orders, idx, *refs):
    parts = refs[:pieces]
    up_v, acted, frame_id, order = refs[pieces : pieces + 4]
    cols_grad, *streams = refs[pieces + 4 : pieces + 9]
    wide, stacked, phases, low_grad, held_v, held_act, held_order, sems = refs[pieces + 9 :]
    rows = parts[0].shape[0]
    own = parts[0].shape[1] - HALO
    length = pieces * own
    frames = length // 8
    late = []
    for source, target in ((order, held_order), (acted, held_act), (up_v, held_v)):
        late.append(pltpu.make_async_copy(source, target, sems.at[len(late)]))
        late[-1].start()
    wide[:, HALO + length :] = jnp.zeros((rows, wide.shape[1] - HALO - length), BF)
    for s in range(pieces):
        peer = idx[1] ^ s
        source = parts[s][:, at(HALO - edge_start(pieces, peer), own, LANES)]
        wide[:, at(HALO + peer * own, own, LANES)] = source

        @pl.when(peer == 0)
        def _():
            wide[:, 0:HALO] = parts[s][:, 0:HALO]

        @pl.when(peer == pieces - 1)
        def _():
            wide[:, HALO + length : 2 * HALO + length] = parts[s][:, own:]

    total = wide.shape[1] // 8
    blocks = total // LANES
    for block in range(blocks):
        stacked[block * rows : (block + 1) * rows, :] = wide[:, block * 1024 : (block + 1) * 1024]
    late[0].wait()
    turned = dot_rt(stacked[...], held_order[...]).astype(BF)
    for block in range(blocks):
        for r in range(8):
            phases[r * rows : (r + 1) * rows, block * LANES : (block + 1) * LANES] = turned[
                block * rows : (block + 1) * rows, r * LANES : (r + 1) * LANES
            ]
    ids = jnp.broadcast_to(frame_id[...], (8, frame_id.shape[1]))
    before = pltpu.roll(ids, 1, axis=1)
    after = pltpu.roll(ids, frame_id.shape[1] - 1, axis=1)
    inside = slice(LANES, LANES + frames)
    left = jnp.where(before == ids, 1.0, 0.0)[0:1, inside]
    right = jnp.where(after == ids, 1.0, 0.0)[0:1, inside]
    lead = HALO // 8
    eighth = 4 * rows
    sample_sum = jnp.zeros((rows, 1), F32)
    for part in range(2):
        base = phases[part * eighth : (part + 1) * eighth, :]
        center = pltpu.roll(base, total - lead, axis=1)[:, 0:frames]
        cols_grad[(4 + 4 * part) * rows : (8 + 4 * part) * rows, :] = center
        partial = jnp.sum(center.astype(F32), axis=1, keepdims=True)
        for r in range(4):
            sample_sum = sample_sum + partial[r * rows : (r + 1) * rows]
        if part == 1:
            moved = pltpu.roll(base, total - lead + 1, axis=1)[:, 0:frames]
            cols_grad[0:eighth, :] = (moved.astype(F32) * left).astype(BF)
        else:
            moved = pltpu.roll(base, total - lead - 1, axis=1)[:, 0:frames]
            cols_grad[12 * rows : 16 * rows, :] = (moved.astype(F32) * right).astype(BF)
    taps = up_v.shape[0]
    channels = up_v.shape[2]
    inner = jnp.zeros((rows, channels), F32)
    late[1].wait()
    grad = dot_rt(cols_grad[...], held_act[...])
    low_grad[...] = grad.astype(BF)
    late[2].wait()
    for k in range(taps):
        inner = inner + grad[k * rows : (k + 1) * rows] * held_v[k]
    inner = jnp.sum(inner, axis=0, keepdims=True)
    bias = jnp.concatenate(
        [to_row(sample_sum, eye_mask(rows)), jnp.zeros((1, channels - rows), F32)], axis=1
    )
    side = channels // 2
    line = lax.broadcasted_iota(jnp.int32, (SUMS, side), 0)
    sums = jnp.zeros((SUMS, side), F32)
    for number, value in enumerate((inner[:, :side], inner[:, side:], bias[:, :side])):
        high = value.astype(BF).astype(F32)
        sums = sums + jnp.where(line == 2 * number, high, 0.0)
        sums = sums + jnp.where(line == 2 * number + 1, value - high, 0.0)
    half = peers // 2
    size = taps * rows // peers
    first = (streams[0].shape[0] - SUMS) // half
    second = 2 * size - first
    streams[0][half * first :, :] = sums.astype(BF)
    streams[1][half * first :, :] = sums.astype(BF)
    for position, s in enumerate(orders[0]):
        target = streams[position // half]
        start = position % half * first
        target[start : start + first, :] = low_grad[at((idx[0] ^ s) * size, first, 16), 0:side]
    for position, s in enumerate(orders[1]):
        target = streams[2 + position // half]
        start = position % half * second
        piece = (idx[0] ^ s) * size
        target[start : start + size, :] = low_grad[at(piece, size, 16), side:]
        if size > first:
            target[start + size : start + second, :] = low_grad[
                at(piece + first, size - first, 16), 0:side
            ]


def input_back_kernel(pieces, order, idx, up_w, cols_grad, keep, send, total):
    total[...] = lax.dot_general(
        up_w[...], cols_grad[...], (((0,), (0,)), ((), ())), preferred_element_type=F32
    ).astype(BF)
    size = total.shape[0] // pieces
    for position, s in enumerate(order):
        target = (keep, send)[position // (pieces // 2)]
        start = position % (pieces // 2) * size
        target[start : start + size, :] = total[at((idx[1] ^ s) * size, size, 16), :]


def join_kernel(idx, keep, got, term, other, next_keep, next_send):
    rows = keep.shape[0] - SUMS
    half, part = rows // 2, term.shape[0] // 2
    total = keep[...].astype(F32) + got[...].astype(F32)
    grads = (term[...].astype(F32) + other[...].astype(F32)).astype(BF)
    for number, target in enumerate((next_keep, next_send)):
        target[0:half, :] = total[number * half : (number + 1) * half].astype(BF)
        target[half : half + part, :] = grads[number * part : (number + 1) * part]
        target[half + part :, :] = total[rows:].astype(BF)


def step_kernel(rows, idx, keep, got, *outs):
    total = keep[...].astype(F32) + got[...].astype(F32)
    grads = total.shape[0] - rows - SUMS
    for number, target in enumerate(outs):
        half, part = rows // 2, grads // 2
        target[0:half, :] = total[number * half : (number + 1) * half].astype(BF)
        start = rows + number * part
        target[half : half + part, :] = total[start : start + part].astype(BF)
        target[half + part :, :] = total[rows + grads :].astype(BF)


def meet_kernel(parts, idx, own, got, out, *sums):
    start = 0
    for count in parts:
        half = count // 2
        for number in range(2):
            here = start + number * half
            there = start + (1 - number) * half
            out[here : here + half, :] = (
                own[here : here + half, :].astype(F32) + got[there : there + half, :].astype(F32)
            ).astype(BF)
        start = start + count
    if sums:
        sums[0][...] = own[start:, :].astype(F32) + got[start:, :].astype(F32)


def whole_kernel(rows, joined, idx, keep, got, *refs):
    *terms, out = refs
    total = keep[...].astype(F32) + got[...].astype(F32)
    if not joined:
        out[...] = total.astype(BF)
        return
    count = terms[0].shape[0]
    out[0:rows, :] = total[0:rows].astype(BF)
    out[rows : rows + count, :] = (terms[0][...].astype(F32) + terms[1][...].astype(F32)).astype(BF)
    out[rows + count :, :] = total[rows:].astype(BF)


def double_kernel(rows, idx, own, got, out):
    grads = own.shape[0] - rows
    out[0:rows, :] = own[0:rows, :]
    out[rows : 2 * rows, :] = got[0:rows, :]
    out[2 * rows : 2 * rows + grads, :] = own[rows:, :]
    out[2 * rows + grads :, :] = got[rows:, :]


def final_kernel(orders, first, idx, *refs):
    streams = refs[:4]
    up_v, up_sq, up_g, inner_sum, dil_v, dil_g, mix_v, mix_g, skip_v, skip_g = refs[4:14]
    up_v_grad, up_g_grad, *outs = refs[14:24]
    whole, blocks_whole, staged, *block_staged, out_sems = refs[24:]
    half = len(orders[0]) // 2
    size = whole.shape[0] // (2 * half)
    side = whole.shape[1] // 2
    second = 2 * size - first
    for position, s in enumerate(orders[0]):
        start = position % half * first
        whole[at((idx[0] ^ s) * size, first, 16), 0:side] = streams[position // half][
            start : start + first, :
        ]
    for position, s in enumerate(orders[1]):
        source = streams[2 + position // half]
        start = position % half * second
        piece = (idx[0] ^ s) * size
        whole[at(piece, size, 16), side:] = source[start : start + size, :]
        if size > first:
            whole[at(piece + first, size - first, 16), 0:side] = source[
                start + size : start + second, :
            ]
    size = blocks_whole.shape[0] // (2 * half)
    for position, s in enumerate(orders[0]):
        start = half * first + position % half * size
        blocks_whole[at((idx[0] ^ s) * size, size, 16), :] = streams[position // half][
            start : start + size, :
        ]
    sent = []

    def ship(source, target):
        sent.append(pltpu.make_async_copy(source, target, out_sems.at[len(sent)]))
        sent[-1].start()

    norm = jnp.sqrt(up_sq[...])
    inner = inner_sum[...]
    scale = up_g[...] / norm
    pull = up_g[...] * inner / (norm * norm * norm)
    rows = up_v.shape[1]
    for k in range(up_v.shape[0]):
        grad = whole[k * rows : (k + 1) * rows, :].astype(F32)
        staged[k] = scale * grad - pull * up_v[k]
        ship(staged.at[k], up_v_grad.at[k])
    up_g_grad[...] = inner / norm
    dil_v_hbm, dil_g_out, dil_b_out, mix_v_hbm, mix_g_out, out_b_out, skip_v_hbm, skip_g_out = outs
    dil_v_out, mix_v_out, skip_v_out = block_staged
    eye = eye_mask(rows)
    blocks = dil_v.shape[0]
    tail = blocks_whole[5 * blocks * rows :, :].astype(F32)
    for j in range(blocks):

        def mat(m):
            start = (5 * j + m) * rows
            return blocks_whole[start : start + rows, :].astype(F32)

        square = jnp.zeros((rows, 1), F32)
        inner = jnp.zeros((rows, 1), F32)
        for k in range(3):
            v = dil_v[j, k]
            square = square + jnp.sum(v * v, axis=1, keepdims=True)
            inner = inner + jnp.sum(v * mat(k), axis=1, keepdims=True)
        norm = jnp.sqrt(square)
        gain = to_col(dil_g[j : j + 1, :], eye)
        for k in range(3):
            dil_v_out[j, k] = gain / norm * mat(k) - gain * inner / (norm**3) * dil_v[j, k]
        ship(dil_v_out.at[j], dil_v_hbm.at[j])
        dil_g_out[j : j + 1, :] = to_row(inner / norm, eye)
        for number, (vref, gref, v_out, v_hbm, g_out) in enumerate(
            (
                (mix_v, mix_g, mix_v_out, mix_v_hbm, mix_g_out),
                (skip_v, skip_g, skip_v_out, skip_v_hbm, skip_g_out),
            )
        ):
            v = vref[j]
            grad = mat(3 + number)
            norm = jnp.sqrt(jnp.sum(v * v, axis=1, keepdims=True))
            inner = jnp.sum(v * grad, axis=1, keepdims=True)
            gain = to_col(gref[j : j + 1, :], eye)
            v_out[j] = gain / norm * grad - gain * inner / (norm**3) * v
            ship(v_out.at[j], v_hbm.at[j])
            g_out[j : j + 1, :] = to_row(inner / norm, eye)
        dil_b_out[j : j + 1, :] = to_row(tail[:, 2 * j : 2 * j + 1], eye)
        out_b_out[j : j + 1, :] = to_row(tail[:, 2 * j + 1 : 2 * j + 2], eye)
    for copy in sent:
        copy.wait()


def place_kernel(pieces, idx, *refs):
    parts, out = refs[:pieces], refs[pieces]
    own = parts[0].shape[1]
    for s in range(pieces):
        out[:, at((idx[1] ^ s) * own, own, LANES)] = parts[s][...]


def stage_kernel(idx, *refs):
    *pairs, sems = refs
    half = len(pairs) // 2
    fetch(list(zip(pairs[:half], pairs[half:])), sems)


def input_kernel(idx, *refs):
    *terms, spectrogram, out = refs
    total = terms[0][...].astype(F32)
    for term in terms[1:]:
        total = total + term[...].astype(F32)
    out[...] = (total * unit(spectrogram[...].astype(F32))[1]).astype(BF)


def local(
    spectrogram_input,
    upsample_direction,
    upsample_magnitude,
    upsample_bias,
    dilated_direction,
    dilated_magnitude,
    dilated_bias,
    pointwise_direction,
    pointwise_magnitude,
    block_output_bias,
    shortcut_direction,
    shortcut_magnitude,
    cotangent,
    silence,
    segments,
):
    pieces, peers = lax.axis_size("chan"), lax.axis_size("tm")
    chan, tm = lax.axis_index("chan"), lax.axis_index("tm")
    in_rows, frames = spectrogram_input.shape
    taps, rows, in_channels = upsample_direction.shape
    blocks = dilated_direction.shape[0]
    channels = dilated_direction.shape[3]
    length = 8 * frames
    own = length // pieces
    width = own + 2 * HALO
    packed_width = 5 * channels + TAIL
    forward = [(k, k + 1) for k in range(peers - 1)]
    backward = [(k + 1, k) for k in range(peers - 1)]
    dma = pltpu.SemaphoreType.DMA
    lead = HALO // 8
    tie = lax.optimization_barrier

    spread = np.arange(8 * LANES)
    order = np.zeros((8 * LANES, 8 * LANES), np.float32)
    order[spread, 8 * (spread % LANES) + spread // LANES] = 1.0
    order = jnp.asarray(order, BF)

    silence_row = silence.reshape(1, length)
    up_g = upsample_magnitude.reshape(1, in_channels)
    edge_rows = in_rows + rows
    ahead, behind = kernel_call(
        edge_kernel,
        [((edge_rows, LANES), BF, "V")] * 2,
        [spectrogram_input, cotangent, silence_row],
        "HHH",
        scratch=[
            pltpu.VMEM((in_rows, LANES), BF),
            pltpu.VMEM((in_rows, LANES), BF),
            pltpu.VMEM((2, rows, HALO), BF),
            pltpu.VMEM((2, 1, HALO), jnp.int32),
            dma((6,)),
        ],
    )
    low_edge = lax.ppermute(ahead, "tm", forward)
    high_edge = lax.ppermute(behind, "tm", backward)
    all_mains = gather_chan(spectrogram_input)
    (up_sq,) = kernel_call(
        square_kernel, [((1, in_channels), F32, "V")], [upsample_direction], "F", micros=2
    )
    block_args = [
        dilated_direction,
        dilated_magnitude,
        dilated_bias,
        pointwise_direction,
        pointwise_magnitude,
        block_output_bias,
        shortcut_direction,
        shortcut_magnitude,
    ]
    sides = jnp.concatenate([low_edge[:in_rows], high_edge[:in_rows]], axis=1)
    block_args, sides = tie((block_args, sides))
    packed_half = ((blocks * rows // 2, packed_width), BF, "V")
    bias_in = upsample_bias.reshape(1, rows)
    packed, near, far, up_g, bias_in = kernel_call(
        prep_kernel,
        [((blocks * rows, packed_width), BF, "V"), packed_half, packed_half]
        + [((1, in_channels), F32, "R"), ((1, rows), F32, "R")],
        [*block_args, up_g, bias_in],
        "FFFFFFFFFF",
        micros=3,
    )
    held_sides = {0: sides}
    for bit in reversed(bits_of(pieces)[1:]):
        for slot in list(held_sides):
            held_sides[slot ^ bit] = swap(held_sides[slot], "chan", bit)
    near, held_sides = tie((near, held_sides))
    for slot in list(held_sides):
        held_sides[slot ^ 1] = swap(held_sides[slot], "chan", 1)
    all_sides = [held_sides[slot] for slot in range(pieces)]
    for bit in bits_of(pieces):
        up_sq = up_sq + swap(up_sq, "chan", bit)
    padded_ids = jnp.pad(segments.astype(F32), LANES, constant_values=-1.0)
    frame_id = lax.dynamic_slice_in_dim(padded_ids, tm * frames, frames + 2 * LANES)
    sample_id = jnp.repeat(
        lax.dynamic_slice_in_dim(
            padded_ids, LANES + tm * frames + chan * (own // 8) - lead, width // 8
        ),
        8,
    ).reshape(1, width)
    frame_id = frame_id.reshape(1, frames + 2 * LANES)
    top = pieces // 2
    near, all_sides[top], up_sq = tie((near, all_sides[top], up_sq))

    count = -(-(frames + 2 * lead) // LANES) * LANES
    count = -(-count // (3 * LANES)) * 3 * LANES
    up_outs = kernel_call(
        functools.partial(up_kernel, pieces),
        [((rows, width), BF, "R")]
        + [((rows, width), BF, "V")] * (pieces - 1)
        + [((in_channels, frames), BF, "H"), ((taps * rows, in_channels), BF, "H")],
        all_mains
        + all_sides
        + [upsample_direction, up_sq, up_g, bias_in, frame_id, order],
        "V" * (2 * pieces) + "HVRRVH",
        scratch=[
            pltpu.VMEM((in_channels, frames + 2 * LANES), BF),
            pltpu.VMEM((3 * in_channels, count), BF),
            pltpu.VMEM((count // LANES * rows, 8 * LANES), BF),
            pltpu.VMEM((rows, 8 * count), BF),
            pltpu.VMEM((in_channels, frames), BF),
            pltpu.VMEM((taps * rows, in_channels), BF),
            pltpu.VMEM(upsample_direction.shape, F32),
            pltpu.VMEM(order.shape, BF),
            dma((2,)),
            dma((2,)),
        ],
        micros=6,
    )
    acted, up_w = up_outs[pieces:]
    chan_bits = bits_of(pieces)
    held_near = {0: near}
    for bit in reversed(chan_bits[1:]):
        for slot in list(held_near):
            held_near[slot ^ bit] = swap(held_near[slot], "chan", bit)
    hidden_parts, held_near, low_edge = tie((list(up_outs[:pieces]), held_near, low_edge))
    cut = kernel_call(
        functools.partial(cut_kernel, pieces),
        [((rows, width), BF, "R")] + [((rows, width), BF, "V")] * (pieces - 1),
        [cotangent, silence_row, low_edge, high_edge],
        "FFVV",
        scratch=[pltpu.VMEM((rows, length + 2 * HALO), BF)],
        micros=2,
    )
    all_hidden = exchange_chan(hidden_parts)
    all_packed = [packed, swap(packed, "chan", 1)]
    for slot in range(2, pieces, 2):
        two = [held_near[slot], swap(held_near[slot], "tm", 1)]
        two, all_hidden[top], cut = tie((two, all_hidden[top], list(cut)))
        all_packed += two + [swap(value, "chan", 1) for value in two]

    plain, dil_t, point_t = kernel_call(
        functools.partial(weight_kernel, pieces, blocks),
        [
            ((blocks, channels, packed_width), BF, "R"),
            ((blocks, channels, 3 * channels), BF, "R"),
            ((blocks, channels, 2 * channels), BF, "R"),
        ],
        all_packed,
        "V" * len(all_packed),
        micros=0.1,
    )
    cut, plain = tie((list(cut), plain))
    all_err = exchange_chan(cut)

    kept_shape = ((blocks, channels, width), BF, "R")
    forward_outs = kernel_call(
        functools.partial(forward_kernel, pieces, blocks),
        [((rows, own), BF, "V")] * pieces + [kept_shape] * 5,
        all_hidden + [plain, sample_id, silence_row],
        "R" + "V" * (pieces - 1) + "RVF",
        scratch=[
            pltpu.VMEM((channels, width), BF),
            pltpu.VMEM((3 * channels, width), BF),
            pltpu.VMEM((2 * channels, width), BF),
            pltpu.VMEM((channels, width), F32),
        ],
        micros=10,
    )
    keep_h, keep_u, keep_m, keep_sh, keep_sc = forward_outs[pieces:]
    activation_parts = list(forward_outs[:pieces])

    backward_outs = kernel_call(
        functools.partial(backward_kernel, pieces),
        [((rows, width - HALO), BF, "V")] * pieces + [kept_shape] * 2,
        all_err + [dil_t, point_t, sample_id, keep_sh, keep_sc],
        "R" + "V" * (pieces - 1) + "RRVRR",
        scratch=[
            pltpu.VMEM((3 * channels, width), BF),
            pltpu.VMEM((channels, width), BF),
        ],
        micros=10,
    )
    errs, inners = backward_outs[pieces:]
    all_low = exchange_chan(list(backward_outs[:pieces]))

    chan_order = order_of(chan_bits)
    tm_bits = bits_of(peers)
    path = [("chan", 1), ("tm", 1)] + [("chan", bit) for bit in chan_bits[1:]]
    path_order = [(0, 0)]
    for axis, bit in reversed(path + [("tm", bit) for bit in tm_bits[1:]]):
        other = [
            (s + bit, t) if axis == "chan" else (s, t + bit) for s, t in path_order
        ]
        path_order = path_order + other
    mats = 5 * blocks + 1
    share = pieces // 2 * mats * rows
    keep, send = kernel_call(
        functools.partial(grad_kernel, pieces, path_order),
        [((share, channels), BF, "V")] * 2,
        [errs, inners, sample_id, keep_h, keep_u, keep_m],
        "RRVRRR",
        scratch=[
            pltpu.VMEM((3 * channels, width), BF),
            pltpu.VMEM((mats, channels, channels), BF),
        ],
        micros=0.1,
    )

    def scatter(keep, send, path):
        for axis, bit in path[:-1]:
            got = swap(send, axis, bit)
            next_shape = ((keep.shape[0] // 2, keep.shape[1]), BF, "V")
            keep, send = kernel_call(halve_kernel, [next_shape] * 2, [keep, got], "VV")
        return keep, swap(send, *path[-1])

    keep, send, all_low[top] = tie((keep, send, all_low[top]))
    got = swap(send, *path[0])
    keep, send = kernel_call(
        halve_kernel, [((share // 2, channels), BF, "V")] * 2, [keep, got], "VV"
    )
    block_terms = scatter(keep, send, path[1:])
    send, all_low = tie((send, all_low))

    turned_bits = tm_bits[1:] + tm_bits[:1]
    orders = (order_of(tm_bits), order_of(turned_bits))
    half = peers // 2
    total_rows = taps * rows
    size = total_rows // peers
    side = in_channels // 2
    first = max(16, size // 2 // 16 * 16)
    second = 2 * size - first
    cols_grad, keep_one, send_one, keep_two, send_two = kernel_call(
        functools.partial(up_back_kernel, pieces, peers, orders),
        [((total_rows, frames), BF, "R")]
        + [((half * first + SUMS, side), BF, "V")] * 2
        + [((half * second, side), BF, "V")] * 2,
        all_low + [upsample_direction, acted, frame_id, order],
        "V" * pieces + "HHVH",
        scratch=[
            pltpu.VMEM((rows, 8 * count), BF),
            pltpu.VMEM((count // LANES * rows, 8 * LANES), BF),
            pltpu.VMEM((8 * rows, count), BF),
            pltpu.VMEM((total_rows, in_channels), BF),
            pltpu.VMEM(upsample_direction.shape, F32),
            pltpu.VMEM((in_channels, frames), BF),
            pltpu.VMEM(order.shape, BF),
            dma((3,)),
        ],
        micros=5,
    )

    piece_rows = pieces // 2 * in_rows
    keep, send = kernel_call(
        functools.partial(input_back_kernel, pieces, chan_order),
        [((piece_rows, frames), BF, "V")] * 2,
        [up_w, cols_grad],
        "FR",
        scratch=[pltpu.VMEM((in_channels, frames), BF)],
        micros=3,
    )
    steps = len(tm_bits)
    block_rows = mats * rows
    one_rows, two_rows = half * first, half * second
    for step in range(steps - 1):
        got_one = swap(send_one, "tm", tm_bits[step])
        got_two = swap(send_two, "tm", turned_bits[step])
        if step == 0:
            got_one, got_two, keep, send = tie((got_one, got_two, keep, send))
            activation_parts, got_one = tie((activation_parts, got_one))
            activation_parts = exchange_chan(activation_parts)
            input_terms = scatter(keep, send, [("chan", bit) for bit in chan_bits])
        else:
            got_one, got_two = tie((got_one, got_two))
        one_rows, two_rows, block_rows = one_rows // 2, two_rows // 2, block_rows // 2
        if step < steps - 2:
            next_shape = ((one_rows + block_rows // 2 + SUMS, side), BF, "V")
            if step == 0:
                keep_one, send_one = kernel_call(
                    join_kernel, [next_shape] * 2, [keep_one, got_one, *block_terms], "VVVV"
                )
            else:
                keep_one, send_one = kernel_call(
                    functools.partial(step_kernel, 2 * one_rows),
                    [next_shape] * 2,
                    [keep_one, got_one],
                    "VV",
                )
            keep_two, send_two = kernel_call(
                halve_kernel, [((two_rows, side), BF, "V")] * 2, [keep_two, got_two], "VV"
            )
    joined = steps == 2
    one_rows, two_rows = 2 * one_rows, 2 * two_rows
    (held_one,) = kernel_call(
        functools.partial(whole_kernel, one_rows, joined),
        [((one_rows + block_rows + SUMS, side), BF, "V")],
        [keep_one, got_one, *(block_terms if joined else ())],
        "VVVV" if joined else "VV",
    )
    (held_two,) = kernel_call(
        functools.partial(whole_kernel, two_rows, False),
        [((two_rows, side), BF, "V")],
        [keep_two, got_two],
        "VV",
    )
    got_one = swap(held_one, "tm", tm_bits[-1])
    got_two = swap(held_two, "tm", turned_bits[-1])
    got_one, got_two, input_terms = tie((got_one, got_two, input_terms))
    own_one, sums = kernel_call(
        functools.partial(meet_kernel, (one_rows, block_rows)),
        [((one_rows + block_rows, side), BF, "V"), ((SUMS, side), F32, "V")],
        [held_one, got_one],
        "VV",
    )
    (own_two,) = kernel_call(
        functools.partial(meet_kernel, (two_rows,)),
        [((two_rows, side), BF, "V")],
        [held_two, got_two],
        "VV",
    )
    for step in reversed(range(steps - 1)):
        got_one = swap(own_one, "tm", tm_bits[step])
        got_two = swap(own_two, "tm", turned_bits[step])
        if step == steps - 2:
            got_one, got_two, activation_parts = tie((got_one, got_two, activation_parts))
        else:
            got_one, got_two = tie((got_one, got_two))
        if step > 0:
            (own_one,) = kernel_call(
                functools.partial(double_kernel, one_rows),
                [((2 * own_one.shape[0], side), BF, "V")],
                [own_one, got_one],
                "VV",
            )
            one_rows = 2 * one_rows
            own_two = jnp.concatenate([own_two, got_two], axis=0)

    pair = sums[0:6:2] + sums[1:6:2]
    inner_sum = pair[0:2].reshape(1, in_channels)
    for bit in chan_bits:
        inner_sum = inner_sum + swap(inner_sum, "chan", bit)

    (input_grad,) = kernel_call(
        input_kernel,
        [((in_rows, frames), BF, "V")],
        [*input_terms, spectrogram_input],
        "VVF",
    )
    (activation,) = kernel_call(
        functools.partial(place_kernel, pieces),
        [((rows, length), BF, "V")],
        activation_parts,
        "V" * pieces,
        micros=2,
    )

    late_args = [
        upsample_direction,
        dilated_direction,
        dilated_magnitude,
        pointwise_direction,
        pointwise_magnitude,
        shortcut_direction,
        shortcut_magnitude,
    ]
    late_args, sums = tie((late_args, sums))
    staged = kernel_call(
        stage_kernel,
        [(arg.shape, arg.dtype, "R") for arg in late_args],
        late_args,
        "H" * len(late_args),
        scratch=[dma((len(late_args),))],
        micros=2,
    )
    final_outs = kernel_call(
        functools.partial(final_kernel, orders, first),
        [
            (upsample_direction.shape, F32, "H"),
            ((1, in_channels), F32, "V"),
            (dilated_direction.shape, F32, "H"),
            (dilated_magnitude.shape, F32, "V"),
            (dilated_bias.shape, F32, "V"),
            (pointwise_direction.shape, F32, "H"),
            (pointwise_magnitude.shape, F32, "V"),
            (block_output_bias.shape, F32, "V"),
            (shortcut_direction.shape, F32, "H"),
            (shortcut_magnitude.shape, F32, "V"),
        ],
        [
            own_one,
            got_one,
            own_two,
            got_two,
            staged[0],
            up_sq,
            up_g,
            inner_sum,
            *staged[1:],
        ],
        "VVVVRVRVRRRRRR",
        scratch=[
            pltpu.VMEM((total_rows, in_channels), BF),
            pltpu.VMEM((mats * rows, channels), BF),
            pltpu.VMEM(upsample_direction.shape, F32),
            pltpu.VMEM(dilated_direction.shape, F32),
            pltpu.VMEM(pointwise_direction.shape, F32),
            pltpu.VMEM(shortcut_direction.shape, F32),
            dma((taps + 3 * blocks,)),
        ],
        micros=5,
    )
    up_v_grad, up_g_grad, dil_v_grad, dil_g_grad, dil_b_grad = final_outs[:5]
    mix_v_grad, mix_g_grad, out_b_grad, skip_v_grad, skip_g_grad = final_outs[5:]
    return (
        activation,
        input_grad,
        up_v_grad,
        up_g_grad.reshape(in_channels),
        pair[2, :rows],
        dil_v_grad,
        dil_g_grad,
        dil_b_grad,
        mix_v_grad,
        mix_g_grad,
        out_b_grad,
        skip_v_grad,
        skip_g_grad,
    )


def solution(mesh):
    placed = (
        P("chan", "tm"),
        P(None, "chan", None),
        P(),
        P("chan"),
        P(None, None, "chan", None),
        P(None, "chan"),
        P(None, "chan"),
        P(None, "chan", None),
        P(None, "chan"),
        P(None, "chan"),
        P(None, "chan", None),
        P(None, "chan"),
        P("chan", "tm"),
        P("tm"),
        P(),
    )
    return jax.shard_map(
        local,
        mesh=mesh,
        in_specs=placed,
        out_specs=(
            P("chan", "tm"),
            P("chan", "tm"),
            P(None, "chan", None),
            P(),
            P("chan"),
            P(None, None, "chan", None),
            P(None, "chan"),
            P(None, "chan"),
            P(None, "chan", None),
            P(None, "chan"),
            P(None, "chan"),
            P(None, "chan", None),
            P(None, "chan"),
        ),
        check_vma=False,
    )
```

profile of v0, /device:TPU:0, one launch (start us, length us, event | category | flops | bytes accessed | tf_op | source)
XLA Modules:
  0.0 148.3 jit_solution(7463725630488834051)
XLA Ops:
  0.6 3.0 %collective-permute-start.1 = (bf16[128,1024]{1,0:T(8,128)(2,1)}, bf16[128,1024]{1,0:T(8,128)(2,1)S(1)}, u32[]{:S(2)}, u32[]{:S(2)}) collective-permute-start(bf16[128,1024]{1,0:T(8,128)(2,1)} %refs_2_.2), channel_id=1, source_target_pairs={{0,2},{1,3},{2,0},{3,1},{4,6},{5,7},{6,4},{7,5},{8,10},{9,11},{10,... | collective-permute-start | bytes 786440 | tf_op jit(solution)/shard_map/ppermute | solution.py:22
  4.5 3.4 %collective-permute-start.3 = (bf16[192,128]{1,0:T(8,128)(2,1)S(1)}, bf16[192,128]{1,0:T(8,128)(2,1)S(1)}, u32[]{:S(2)}, u32[]{:S(2)}) collective-permute-start(bf16[192,128]{1,0:T(8,128)(2,1)S(1)} %get-tuple-element.155), channel_id=1, source_target_pairs={{0,4},{4,8},{8,12},{12,16},{16,20},{20,24},{24,28},{1,5},{5,9},{9,... | collective-permute-start | bytes 147464 | tf_op jit(solution)/shard_map/ppermute | solution.py:819
  14.7 2.4 %shard_map.256 = (bf16[192,1408]{1,0:T(8,128)(2,1)S(1)}, bf16[96,1408]{1,0:T(8,128)(2,1)S(1)}, bf16[96,1408]{1,0:T(8,128)(2,1)}, f32[1,512]{1,0:T(1,128)S(1)}, f32[1,64]{1,0:T(1,128)S(1)}) custom-call(f32[3,3,64,256]{3,2,1,0:T(8,128)} %refs_1_.3, f32[3,64]{1,0:T(4,128)} %refs_2_.3, f32[3,64]{1,0:T(4,128)} %refs_2_.1, f32[3,64,256]{2,1,0:T(8,128)} %refs_3_.1, ...), custom_call_target="tpu_custom_call" | custom-call | flops 3300000000 | tf_op jit(solution)/shard_map/pallas_call | solution.py:91
  19.9 6.0 %shard_map.258 = (bf16[64,2304]{1,0:T(8,128)(2,1)S(1)}, bf16[64,2304]{1,0:T(8,128)(2,1)S(1)}, bf16[64,2304]{1,0:T(8,128)(2,1)S(1)}, bf16[64,2304]{1,0:T(8,128)(2...) custom-call(bf16[128,1024]{1,0:T(8,128)(2,1)S(1)} %copy-done.2, ...), custom_call_target="tpu_custom_call" | custom-call | flops 6600000000 | tf_op jit(solution)/shard_map/pallas_call | solution.py:91
  28.3 2.4 %collective-permute-start.11 = (bf16[96,1408]{1,0:T(8,128)(2,1)S(1)}, bf16[96,1408]{1,0:T(8,128)(2,1)S(1)}, u32[]{:S(2)}, u32[]{:S(2)}) collective-permute-start(bf16[96,1408]{1,0:T(8,128)(2,1)S(1)} %collective-permute-done.10.refs_2_), channel_id=1, source_target_pairs={{0,4},{4,0},{8,12},{12,8},{16,20},{20,16},{24,28},{28,24},{1,5},{5... | collective-permute-start | bytes 811016 | tf_op jit(solution)/shard_map/ppermute | solution.py:22
  43.7 11.1 %shard_map.261 = (bf16[64,2048]{1,0:T(8,128)(2,1)S(1)}, bf16[64,2048]{1,0:T(8,128)(2,1)S(1)}, bf16[64,2048]{1,0:T(8,128)(2,1)S(1)}, bf16[64,2048]{1,0:T(8,128)(2...) custom-call(bf16[64,2304]{1,0:T(8,128)(2,1)S(1)} %copy-done.6, ...), custom_call_target="tpu_custom_call" | custom-call | flops 11000000512 | tf_op jit(solution)/shard_map/pallas_call | solution.py:91
  56.3 5.6 %shard_map.262 = (bf16[64,2176]{1,0:T(8,128)(2,1)S(1)}, bf16[64,2176]{1,0:T(8,128)(2,1)S(1)}, bf16[64,2176]{1,0:T(8,128)(2,1)S(1)}, bf16[64,2176]{1,0:T(8,128)(2...) custom-call(bf16[64,2304]{1,0:T(8,128)(2,1)S(1)} %copy-done.4, ...), custom_call_target="tpu_custom_call" | custom-call | flops 11000000512 | tf_op jit(solution)/shard_map/pallas_call | solution.py:91
  62.3 5.4 %shard_map.263 = (bf16[2048,256]{1,0:T(8,128)(2,1)S(1)}, bf16[2048,256]{1,0:T(8,128)(2,1)S(1)}) custom-call(bf16[3,256,2304]{2,1,0:T(8,128)(2,1)S(1)} %get-tuple-element.207.refs_0_, bf16[3,256,2304]{2,1,0:T(8,128)(2,1)S(1)} %get-tuple-element.208.refs_1_, f32[1,2304]{1,0:T(1,128)S(1)} %reshape_reshape.3.refs_5_.refs_6_.refs_2_, ...), custom_call_target="tpu_custom_call" | custom-call | flops 110000000 | tf_op jit(solution)/shard_map/pallas_call | solution.py:91
  67.7 3.1 %collective-permute-done.21.refs_2_ = bf16[64,2176]{1,0:T(8,128)(2,1)S(1)} collective-permute-done((bf16[64,2176]{1,0:T(8,128)(2,1)S(1)}, bf16[64,2176]{1,0:T(8,128)(2,1)S(1)}, u32[]{:S(2)}, u32[]{:S(2)}) %collective-permute-start.21) | collective-permute-done | bytes 278560 | tf_op jit(solution)/shard_map/ppermute | solution.py:22
  71.3 2.1 %collective-permute-done.22.refs_1_ = bf16[2048,256]{1,0:T(8,128)(2,1)S(1)} collective-permute-done((bf16[2048,256]{1,0:T(8,128)(2,1)S(1)}, bf16[2048,256]{1,0:T(8,128)(2,1)S(1)}, u32[]{:S(2)}, u32[]{:S(2)}) %collective-permute-start.22) | collective-permute-done | bytes 1048608 | tf_op jit(solution)/shard_map/ppermute | solution.py:22
  73.7 2.5 %collective-permute-start.27 = (bf16[1024,256]{1,0:T(8,128)(2,1)S(1)}, bf16[1024,256]{1,0:T(8,128)(2,1)S(1)}, u32[]{:S(2)}, u32[]{:S(2)}) collective-permute-start(bf16[1024,256]{1,0:T(8,128)(2,1)S(1)} %get-tuple-element.217), channel_id=1, source_target_pairs={{0,4},{4,0},{8,12},{12,8},{16,20},{20,16},{24,28},{28,24},{1,5},{5... | collective-permute-start | bytes 1572872 | tf_op jit(solution)/shard_map/ppermute | solution.py:22
  76.2 3.9 %collective-permute-done.24.refs_3_ = bf16[64,2176]{1,0:T(8,128)(2,1)S(1)} collective-permute-done((bf16[64,2176]{1,0:T(8,128)(2,1)S(1)}, bf16[64,2176]{1,0:T(8,128)(2,1)S(1)}, u32[]{:S(2)}, u32[]{:S(2)}) %collective-permute-start.24) | collective-permute-done | bytes 278560 | tf_op jit(solution)/shard_map/ppermute | solution.py:22
  80.1 5.1 %shard_map.265 = (bf16[1024,1024]{1,0:T(8,128)(2,1)S(1)}, bf16[272,256]{1,0:T(8,128)(2,1)S(1)}, bf16[272,256]{1,0:T(8,128)(2,1)S(1)}, bf16[768,256]{1,0:T(8,128)(2,1)S(1)}, bf16[768,256]{1,0:T(8,128)(2,1)S(1)}) custom-call(bf16[64,2176]{1,0:T(8,128)(2,1)S(1)} %get-tuple-element.222.refs_0_, bf16[64,2176]{1,0:T(8,128)(2,1)S(1)} %collective-permute-done.23.refs_1_, ...), custom_call_target="tpu_custom_call" | custom-call | flops 5500000256 | tf_op jit(solution)/shard_map/pallas_call | solution.py:91
  85.2 2.5 %collective-permute-start.25 = (bf16[272,256]{1,0:T(8,128)(2,1)S(1)}, bf16[272,256]{1,0:T(8,128)(2,1)S(1)}, u32[]{:S(2)}, u32[]{:S(2)}) collective-permute-start(bf16[272,256]{1,0:T(8,128)(2,1)S(1)} %get-tuple-element.232), channel_id=1, source_target_pairs={{0,4},{4,0},{8,12},{12,8},{16,20},{20,16},{24,28},{28,24},{1,5},{5... | collective-permute-start | bytes 417800 | tf_op jit(solution)/shard_map/ppermute | solution.py:22
  90.2 2.6 %shard_map.266 = (bf16[256,1024]{1,0:T(8,128)(2,1)S(1)}, bf16[256,1024]{1,0:T(8,128)(2,1)S(1)}) custom-call(bf16[1024,512]{1,0:T(8,128)(2,1)} %get-tuple-element.234.refs_0_, bf16[1024,1024]{1,0:T(8,128)(2,1)S(1)} %get-tuple-element.235.refs_1_), custom_call_target="tpu_custom_call" | custom-call | flops 3300000000 | tf_op jit(solution)/shard_map/pallas_call | solution.py:91
  92.9 5.9 %collective-permute-done.26.refs_1_ = bf16[768,256]{1,0:T(8,128)(2,1)S(1)} collective-permute-done((bf16[768,256]{1,0:T(8,128)(2,1)S(1)}, bf16[768,256]{1,0:T(8,128)(2,1)S(1)}, u32[]{:S(2)}, u32[]{:S(2)}) %collective-permute-start.26) | collective-permute-done | bytes 393248 | tf_op jit(solution)/shard_map/ppermute | solution.py:22
  100.6 2.0 %collective-permute-start.30 = (bf16[384,256]{1,0:T(8,128)(2,1)S(1)}, bf16[384,256]{1,0:T(8,128)(2,1)S(1)}, u32[]{:S(2)}, u32[]{:S(2)}) collective-permute-start(bf16[384,256]{1,0:T(8,128)(2,1)S(1)} %get-tuple-element.247), channel_id=1, source_target_pairs={{0,16},{4,20},{8,24},{12,28},{16,0},{20,4},{24,8},{28,12},{1,17},{... | collective-permute-start | bytes 589832 | tf_op jit(solution)/shard_map/ppermute | solution.py:22
  104.0 8.8 %collective-permute-done.30.refs_1_ = bf16[384,256]{1,0:T(8,128)(2,1)S(1)} collective-permute-done((bf16[384,256]{1,0:T(8,128)(2,1)S(1)}, bf16[384,256]{1,0:T(8,128)(2,1)S(1)}, u32[]{:S(2)}, u32[]{:S(2)}) %collective-permute-start.30) | collective-permute-done | bytes 196640 | tf_op jit(solution)/shard_map/ppermute | solution.py:22
  116.0 3.6 %collective-permute-done.32.refs_1_ = bf16[384,256]{1,0:T(8,128)(2,1)S(1)} collective-permute-done((bf16[384,256]{1,0:T(8,128)(2,1)S(1)}, bf16[384,256]{1,0:T(8,128)(2,1)S(1)}, u32[]{:S(2)}, u32[]{:S(2)}) %collective-permute-start.32) | collective-permute-done | bytes 196640 | tf_op jit(solution)/shard_map/ppermute | solution.py:22
  119.6 3.8 %collective-permute-done.31.refs_1_ = bf16[400,256]{1,0:T(8,128)(2,1)S(1)} collective-permute-done((bf16[400,256]{1,0:T(8,128)(2,1)S(1)}, bf16[400,256]{1,0:T(8,128)(2,1)S(1)}, u32[]{:S(2)}, u32[]{:S(2)}) %collective-permute-start.31) | collective-permute-done | bytes 204832 | tf_op jit(solution)/shard_map/ppermute | solution.py:22
  123.6 5.4 %collective-permute-start.35 = (bf16[384,256]{1,0:T(8,128)(2,1)S(1)}, bf16[384,256]{1,0:T(8,128)(2,1)S(1)}, u32[]{:S(2)}, u32[]{:S(2)}) collective-permute-start(bf16[384,256]{1,0:T(8,128)(2,1)S(1)} %get-tuple-element.256.refs_0_), channel_id=1, source_target_pairs={{0,8},{4,12},{8,0},{12,4},{16,24},{20,28},{24,16},{28,20},{1,9},{5... | collective-permute-start | bytes 589832 | tf_op jit(solution)/shard_map/ppermute | solution.py:22
  129.6 4.9 %collective-permute-done.36 = bf16[384,256]{1,0:T(8,128)(2,1)S(1)} collective-permute-done((bf16[384,256]{1,0:T(8,128)(2,1)S(1)}, bf16[384,256]{1,0:T(8,128)(2,1)S(1)}, u32[]{:S(2)}, u32[]{:S(2)}) %collective-permute-start.36) | collective-permute-done | bytes 196640 | tf_op jit(solution)/shard_map/ppermute | solution.py:22
  139.7 1.9 %shard_map.276 = bf16[128,1024]{1,0:T(8,128)(2,1)} custom-call(bf16[128,1024]{1,0:T(8,128)(2,1)S(1)} %get-tuple-element.266.refs_0_, bf16[128,1024]{1,0:T(8,128)(2,1)S(1)} %collective-permute-done.34.refs_1_, bf16[128,1024]{1,0:T(8,128)(2,1)} %refs_2_.2), custom_call_target="tpu_custom_call" | custom-call | flops 1100000000 | tf_op jit(solution)/shard_map/pallas_call | solution.py:91
  145.3 2.9 %shard_map.279 = (f32[16,64,512]{2,1,0:T(8,128)}, f32[1,512]{1,0:T(1,128)}, f32[3,3,64,256]{3,2,1,0:T(8,128)}, f32[3,64]{1,0:T(4,128)}, f32[3,64]{1,0:T(4,128)},...) custom-call(bf16[768,256]{1,0:T(8,128)(2,1)S(1)} %shard_map.277.refs, ...), custom_call_target="tpu_custom_call" | custom-call | flops 5500000256 | tf_op jit(solution)/shard_map/pallas_call | solution.py:91
  (125 shorter events, 46.9 us)
Async XLA Ops:
  0.6 14.1 %collective-permute-start.1 = (bf16[128,1024]{1,0:T(8,128)(2,1)}, bf16[128,1024]{1,0:T(8,128)(2,1)S(1)}, u32[]{:S(2)}, u32[]{:S(2)}) collective-permute-start(bf16[128,1024]{1,0:T(8,128)(2,1)} %refs_2_.2), channel_id=1, source_target_pairs={{0,2},{1,3},{2,0},{3,1},{4,6},{5,7},{6,4},{7,5},{8,10},{9,11},{10,... | collective-permute-start | bytes 786440 | tf_op jit(solution)/shard_map/ppermute | solution.py:22
  27.5 9.9 %collective-permute-start.12 = (bf16[64,2304]{1,0:T(8,128)(2,1)S(1)}, bf16[64,2304]{1,0:T(8,128)(2,1)S(1)}, u32[]{:S(2)}, u32[]{:S(2)}) collective-permute-start(bf16[64,2304]{1,0:T(8,128)(2,1)S(1)} %get-tuple-element.180), channel_id=1, source_target_pairs={{0,2},{1,3},{2,0},{3,1},{4,6},{5,7},{6,4},{7,5},{8,10},{9,11},{10,... | collective-permute-start | bytes 884744 | tf_op jit(solution)/shard_map/ppermute | solution.py:22
  30.7 9.1 %collective-permute-start.13 = (bf16[192,1408]{1,0:T(8,128)(2,1)S(1)}, bf16[192,1408]{1,0:T(8,128)(2,1)S(1)}, u32[]{:S(2)}, u32[]{:S(2)}) collective-permute-start(bf16[192,1408]{1,0:T(8,128)(2,1)S(1)} %get-tuple-element.190.refs_0_), channel_id=1, source_target_pairs={{0,1},{1,0},{2,3},{3,2},{4,5},{5,4},{6,7},{7,6},{8,9},{9,8},{10,11... | collective-permute-start | bytes 1622024 | tf_op jit(solution)/shard_map/ppermute | solution.py:22
  30.7 12.0 %collective-permute-start.19 = (bf16[64,2304]{1,0:T(8,128)(2,1)S(1)}, bf16[64,2304]{1,0:T(8,128)(2,1)}, u32[]{:S(2)}, u32[]{:S(2)}) collective-permute-start(bf16[64,2304]{1,0:T(8,128)(2,1)S(1)} %get-tuple-element.201), channel_id=1, source_target_pairs={{0,1},{1,0},{2,3},{3,2},{4,5},{5,4},{6,7},{7,6},{8,9},{9,8},{10,11... | collective-permute-start | bytes 884744 | tf_op jit(solution)/shard_map/ppermute | solution.py:22
  31.2 11.5 %collective-permute-start.20 = (bf16[64,2304]{1,0:T(8,128)(2,1)S(1)}, bf16[64,2304]{1,0:T(8,128)(2,1)}, u32[]{:S(2)}, u32[]{:S(2)}) collective-permute-start(bf16[64,2304]{1,0:T(8,128)(2,1)S(1)} %get-tuple-element.203), channel_id=1, source_target_pairs={{0,3},{1,2},{2,1},{3,0},{4,7},{5,6},{6,5},{7,4},{8,11},{9,10},{10,... | collective-permute-start | bytes 884744 | tf_op jit(solution)/shard_map/ppermute | solution.py:22
  40.8 14.0 %collective-permute-start.16 = (bf16[64,2304]{1,0:T(8,128)(2,1)}, bf16[64,2304]{1,0:T(8,128)(2,1)S(1)}, u32[]{:S(2)}, u32[]{:S(2)}) collective-permute-start(bf16[64,2304]{1,0:T(8,128)(2,1)} %copy-done.1), channel_id=1, source_target_pairs={{0,1},{1,0},{2,3},{3,2},{4,5},{5,4},{6,7},{7,6},{8,9},{9,8},{10,11... | collective-permute-start | bytes 884744 | tf_op jit(solution)/shard_map/ppermute | solution.py:22
  40.8 14.0 %collective-permute-start.17 = (bf16[64,2304]{1,0:T(8,128)(2,1)}, bf16[64,2304]{1,0:T(8,128)(2,1)S(1)}, u32[]{:S(2)}, u32[]{:S(2)}) collective-permute-start(bf16[64,2304]{1,0:T(8,128)(2,1)} %copy-done), channel_id=1, source_target_pairs={{0,2},{1,3},{2,0},{3,1},{4,6},{5,7},{6,4},{7,5},{8,10},{9,11},{10,... | collective-permute-start | bytes 884744 | tf_op jit(solution)/shard_map/ppermute | solution.py:22
  41.3 15.1 %collective-permute-start.18 = (bf16[64,2304]{1,0:T(8,128)(2,1)S(1)}, bf16[64,2304]{1,0:T(8,128)(2,1)S(1)}, u32[]{:S(2)}, u32[]{:S(2)}) collective-permute-start(bf16[64,2304]{1,0:T(8,128)(2,1)S(1)} %get-tuple-element.197), channel_id=1, source_target_pairs={{0,3},{1,2},{2,1},{3,0},{4,7},{5,6},{6,5},{7,4},{8,11},{9,10},{10,... | collective-permute-start | bytes 884744 | tf_op jit(solution)/shard_map/ppermute | solution.py:22
  61.9 8.9 %collective-permute-start.21 = (bf16[64,2176]{1,0:T(8,128)(2,1)S(1)}, bf16[64,2176]{1,0:T(8,128)(2,1)S(1)}, u32[]{:S(2)}, u32[]{:S(2)}) collective-permute-start(bf16[64,2176]{1,0:T(8,128)(2,1)S(1)} %get-tuple-element.214), channel_id=1, source_target_pairs={{0,2},{1,3},{2,0},{3,1},{4,6},{5,7},{6,4},{7,5},{8,10},{9,11},{10,... | collective-permute-start | bytes 835592 | tf_op jit(solution)/shard_map/ppermute | solution.py:22
  73.7 15.5 %collective-permute-start.27 = (bf16[1024,256]{1,0:T(8,128)(2,1)S(1)}, bf16[1024,256]{1,0:T(8,128)(2,1)S(1)}, u32[]{:S(2)}, u32[]{:S(2)}) collective-permute-start(bf16[1024,256]{1,0:T(8,128)(2,1)S(1)} %get-tuple-element.217), channel_id=1, source_target_pairs={{0,4},{4,0},{8,12},{12,8},{16,20},{20,16},{24,28},{28,24},{1,5},{5... | collective-permute-start | bytes 1572872 | tf_op jit(solution)/shard_map/ppermute | solution.py:22
  87.7 11.0 %collective-permute-start.26 = (bf16[768,256]{1,0:T(8,128)(2,1)S(1)}, bf16[768,256]{1,0:T(8,128)(2,1)S(1)}, u32[]{:S(2)}, u32[]{:S(2)}) collective-permute-start(bf16[768,256]{1,0:T(8,128)(2,1)S(1)} %get-tuple-element.233), channel_id=1, source_target_pairs={{0,8},{4,12},{8,0},{12,4},{16,24},{20,28},{24,16},{28,20},{1,9},{5... | collective-permute-start | bytes 1179656 | tf_op jit(solution)/shard_map/ppermute | solution.py:22
  89.4 9.3 %collective-permute-start.28 = (bf16[512,256]{1,0:T(8,128)(2,1)S(1)}, bf16[512,256]{1,0:T(8,128)(2,1)S(1)}, u32[]{:S(2)}, u32[]{:S(2)}) collective-permute-start(bf16[512,256]{1,0:T(8,128)(2,1)S(1)} %get-tuple-element.242), channel_id=1, source_target_pairs={{0,2},{1,3},{2,0},{3,1},{4,6},{5,7},{6,4},{7,5},{8,10},{9,11},{10,... | collective-permute-start | bytes 786440 | tf_op jit(solution)/shard_map/ppermute | solution.py:22
  98.8 14.0 %collective-permute-start.29 = (bf16[400,256]{1,0:T(8,128)(2,1)S(1)}, bf16[400,256]{1,0:T(8,128)(2,1)S(1)}, u32[]{:S(2)}, u32[]{:S(2)}) collective-permute-start(bf16[400,256]{1,0:T(8,128)(2,1)S(1)} %get-tuple-element.244), channel_id=1, source_target_pairs={{0,8},{4,12},{8,0},{12,4},{16,24},{20,28},{24,16},{28,20},{1,9},{5... | collective-permute-start | bytes 614408 | tf_op jit(solution)/shard_map/ppermute | solution.py:22
  100.6 12.3 %collective-permute-start.30 = (bf16[384,256]{1,0:T(8,128)(2,1)S(1)}, bf16[384,256]{1,0:T(8,128)(2,1)S(1)}, u32[]{:S(2)}, u32[]{:S(2)}) collective-permute-start(bf16[384,256]{1,0:T(8,128)(2,1)S(1)} %get-tuple-element.247), channel_id=1, source_target_pairs={{0,16},{4,20},{8,24},{12,28},{16,0},{20,4},{24,8},{28,12},{1,17},{... | collective-permute-start | bytes 589832 | tf_op jit(solution)/shard_map/ppermute | solution.py:22
  102.7 12.7 %collective-permute-start.34 = (bf16[128,1024]{1,0:T(8,128)(2,1)S(1)}, bf16[128,1024]{1,0:T(8,128)(2,1)S(1)}, u32[]{:S(2)}, u32[]{:S(2)}) collective-permute-start(bf16[128,1024]{1,0:T(8,128)(2,1)S(1)} %get-tuple-element.254), channel_id=1, source_target_pairs={{0,2},{1,3},{2,0},{3,1},{4,6},{5,7},{6,4},{7,5},{8,10},{9,11},{10,... | collective-permute-start | bytes 786440 | tf_op jit(solution)/shard_map/ppermute | solution.py:22
  112.9 10.5 %collective-permute-start.31 = (bf16[400,256]{1,0:T(8,128)(2,1)S(1)}, bf16[400,256]{1,0:T(8,128)(2,1)S(1)}, u32[]{:S(2)}, u32[]{:S(2)}) collective-permute-start(bf16[400,256]{1,0:T(8,128)(2,1)S(1)} %shard_map.270.refs_0_), channel_id=1, source_target_pairs={{0,16},{4,20},{8,24},{12,28},{16,0},{20,4},{24,8},{28,12},{1,17},{... | collective-permute-start | bytes 614408 | tf_op jit(solution)/shard_map/ppermute | solution.py:22
  114.2 15.4 %collective-permute-start.37 = (bf16[64,2048]{1,0:T(8,128)(2,1)S(1)}, bf16[64,2048]{1,0:T(8,128)(2,1)S(1)}, u32[]{:S(2)}, u32[]{:S(2)}) collective-permute-start(bf16[64,2048]{1,0:T(8,128)(2,1)S(1)} %get-tuple-element.259), channel_id=1, source_target_pairs={{0,1},{1,0},{2,3},{3,2},{4,5},{5,4},{6,7},{7,6},{8,9},{9,8},{10,11... | collective-permute-start | bytes 786440 | tf_op jit(solution)/shard_map/ppermute | solution.py:22
  114.2 15.4 %collective-permute-start.38 = (bf16[64,2048]{1,0:T(8,128)(2,1)S(1)}, bf16[64,2048]{1,0:T(8,128)(2,1)S(1)}, u32[]{:S(2)}, u32[]{:S(2)}) collective-permute-start(bf16[64,2048]{1,0:T(8,128)(2,1)S(1)} %get-tuple-element.260), channel_id=1, source_target_pairs={{0,2},{1,3},{2,0},{3,1},{4,6},{5,7},{6,4},{7,5},{8,10},{9,11},{10,... | collective-permute-start | bytes 786440 | tf_op jit(solution)/shard_map/ppermute | solution.py:22
  115.4 14.1 %collective-permute-start.39 = (bf16[64,2048]{1,0:T(8,128)(2,1)S(1)}, bf16[64,2048]{1,0:T(8,128)(2,1)S(1)}, u32[]{:S(2)}, u32[]{:S(2)}) collective-permute-start(bf16[64,2048]{1,0:T(8,128)(2,1)S(1)} %get-tuple-element.261), channel_id=1, source_target_pairs={{0,3},{1,2},{2,1},{3,0},{4,7},{5,6},{6,5},{7,4},{8,11},{9,10},{10,... | collective-permute-start | bytes 786440 | tf_op jit(solution)/shard_map/ppermute | solution.py:22
  123.5 11.0 %collective-permute-start.36 = (bf16[384,256]{1,0:T(8,128)(2,1)S(1)}, bf16[384,256]{1,0:T(8,128)(2,1)S(1)}, u32[]{:S(2)}, u32[]{:S(2)}) collective-permute-start(bf16[384,256]{1,0:T(8,128)(2,1)S(1)} %shard_map.274), channel_id=1, source_target_pairs={{0,16},{4,20},{8,24},{12,28},{16,0},{20,4},{24,8},{28,12},{1,17},{... | collective-permute-start | bytes 589832 | tf_op jit(solution)/shard_map/ppermute | solution.py:22
  123.6 10.9 %collective-permute-start.35 = (bf16[384,256]{1,0:T(8,128)(2,1)S(1)}, bf16[384,256]{1,0:T(8,128)(2,1)S(1)}, u32[]{:S(2)}, u32[]{:S(2)}) collective-permute-start(bf16[384,256]{1,0:T(8,128)(2,1)S(1)} %get-tuple-element.256.refs_0_), channel_id=1, source_target_pairs={{0,8},{4,12},{8,0},{12,4},{16,24},{20,28},{24,16},{28,20},{1,9},{5... | collective-permute-start | bytes 589832 | tf_op jit(solution)/shard_map/ppermute | solution.py:22
  129.5 8.8 %collective-permute-start.42 = (f32[1,512]{1,0:T(1,128)S(1)}, f32[1,512]{1,0:T(1,128)S(1)}, u32[]{:S(2)}, u32[]{:S(2)}) collective-permute-start(f32[1,512]{1,0:T(1,128)S(1)} %bitcast.10), channel_id=1, source_target_pairs={{0,1},{1,0},{2,3},{3,2},{4,5},{5,4},{6,7},{7,6},{8,9},{9,8},{10,11... | collective-permute-start | bytes 6152 | tf_op jit(solution)/shard_map/ppermute | solution.py:22
  134.6 9.5 %collective-permute-start.41 = (bf16[768,256]{1,0:T(8,128)(2,1)S(1)}, bf16[768,256]{1,0:T(8,128)(2,1)S(1)}, u32[]{:S(2)}, u32[]{:S(2)}) collective-permute-start(bf16[768,256]{1,0:T(8,128)(2,1)S(1)} %pad_maximum_fusion.refs_2_), channel_id=1, source_target_pairs={{0,8},{4,12},{8,0},{12,4},{16,24},{20,28},{24,16},{28,20},{1,9},{5... | collective-permute-start | bytes 1179656 | tf_op jit(solution)/shard_map/ppermute | solution.py:22
  135.7 9.6 %collective-permute-start.40 = (bf16[768,256]{1,0:T(8,128)(2,1)S(1)}, bf16[768,256]{1,0:T(8,128)(2,1)S(1)}, u32[]{:S(2)}, u32[]{:S(2)}) collective-permute-start(bf16[768,256]{1,0:T(8,128)(2,1)S(1)} %shard_map.277.refs_0_), channel_id=1, source_target_pairs={{0,4},{4,0},{8,12},{12,8},{16,20},{20,16},{24,28},{28,24},{1,5},{5... | collective-permute-start | bytes 1179656 | tf_op jit(solution)/shard_map/ppermute | solution.py:22
  (28 other events, 129.4 us)
where the time goes:
time: 150 us; the launch traced here: 148 us
  Pallas kernels  52 us (35%)
  waiting for transfers between devices  45.9 us (31%)
  starting transfers between devices  42.7 us (28%)
  local copies, waits for them, and re-layouts  6.36 us (4%)
    pallas_call x25, Pallas kernels, kernel_call(): pl.pallas_call(wrapped, out_shape=tuple(out_shape), in_specs=in_specs, ou...  52 us
    ppermute x42, waiting for transfers between devices, swap(): return lax.ppermute(values, axis, [(k, k ^ bit) for k in range(count)])  44.8 us
    ppermute x42, starting transfers between devices, swap(): return lax.ppermute(values, axis, [(k, k ^ bit) for k in range(count)])  37.9 us
    unnamed x18, local copies, waits for them, and re-layouts  3.84 us
    ppermute x1, starting transfers between devices, local(): low_edge = lax.ppermute(ahead, 'tm', forward)  3.43 us
  transfers between devices with their start and end apart: 44, of which 20 were waited for; matrix products, arithmetic and copies ran while one was open for 2% of the time, Pallas kernels for 29%

commit v1 on v0

--- a/solution.py
+++ b/solution.py
@@ -1033,6 +1033,8 @@
         scratch=[pltpu.VMEM((in_channels, frames), BF)],
         micros=3,
     )
+    keep, send_one = tie((keep, send_one))
+
     steps = len(tm_bits)
     block_rows = mats * rows
     one_rows, two_rows = half * first, half * second

time: 150 us -> 146 us (0.973)
  waiting for transfers between devices: 45.9 us -> 43 us
    ppermute x42, waiting for transfers between devices: 44.8 us -> 41.9 us  [swap(): return lax.ppermute(values, axis, [(k, k ^ bit) for k in range(count)])]
  transfers between devices with their start and end apart: 44 -> 44, of which waited for: 20 -> 22; matrix products, arithmetic and copies ran while one was open for 2% -> 2% of each run, Pallas kernels for 29% -> 30%
where the time goes in v1:
time: 146 us
  Pallas kernels  52.1 us (36%)
  starting transfers between devices  43.1 us (30%)
  waiting for transfers between devices  43 us (29%)
  local copies, waits for them, and re-layouts  6.36 us (4%)
    pallas_call x25, Pallas kernels, kernel_call(): pl.pallas_call(wrapped, out_shape=tuple(out_shape), in_specs=in_specs, ou...  52.1 us
    ppermute x42, waiting for transfers between devices, swap(): return lax.ppermute(values, axis, [(k, k ^ bit) for k in range(count)])  41.9 us
    ppermute x42, starting transfers between devices, swap(): return lax.ppermute(values, axis, [(k, k ^ bit) for k in range(count)])  38.2 us
    unnamed x18, local copies, waits for them, and re-layouts  3.84 us
    ppermute x1, starting transfers between devices, local(): low_edge = lax.ppermute(ahead, 'tm', forward)  3.43 us
  transfers between devices with their start and end apart: 44, of which 22 were waited for; matrix products, arithmetic and copies ran while one was open for 2% of the time, Pallas kernels for 30%

profile of v1, /device:TPU:0, one launch (start us, length us, event | category | flops | bytes accessed | tf_op | source)
XLA Modules:
  0.0 145.8 jit_solution(17540920091669924118)
XLA Ops:
  0.6 3.0 %collective-permute-start.1 = (bf16[128,1024]{1,0:T(8,128)(2,1)}, bf16[128,1024]{1,0:T(8,128)(2,1)S(1)}, u32[]{:S(2)}, u32[]{:S(2)}) collective-permute-start(bf16[128,1024]{1,0:T(8,128)(2,1)} %refs_2_.2), channel_id=1, source_target_pairs={{0,2},{1,3},{2,0},{3,1},{4,6},{5,7},{6,4},{7,5},{8,10},{9,11},{10,... | collective-permute-start | bytes 786440 | tf_op jit(solution)/shard_map/ppermute | solution.py:22
  4.5 3.4 %collective-permute-start.3 = (bf16[192,128]{1,0:T(8,128)(2,1)S(1)}, bf16[192,128]{1,0:T(8,128)(2,1)S(1)}, u32[]{:S(2)}, u32[]{:S(2)}) collective-permute-start(bf16[192,128]{1,0:T(8,128)(2,1)S(1)} %get-tuple-element.157), channel_id=1, source_target_pairs={{0,4},{4,8},{8,12},{12,16},{16,20},{20,24},{24,28},{1,5},{5,9},{9,... | collective-permute-start | bytes 147464 | tf_op jit(solution)/shard_map/ppermute | solution.py:819
  14.7 2.4 %shard_map.256 = (bf16[192,1408]{1,0:T(8,128)(2,1)S(1)}, bf16[96,1408]{1,0:T(8,128)(2,1)S(1)}, bf16[96,1408]{1,0:T(8,128)(2,1)}, f32[1,512]{1,0:T(1,128)S(1)}, f32[1,64]{1,0:T(1,128)S(1)}) custom-call(f32[3,3,64,256]{3,2,1,0:T(8,128)} %refs_1_.3, f32[3,64]{1,0:T(4,128)} %refs_2_.3, f32[3,64]{1,0:T(4,128)} %refs_2_.1, f32[3,64,256]{2,1,0:T(8,128)} %refs_3_.1, ...), custom_call_target="tpu_custom_call" | custom-call | flops 3300000000 | tf_op jit(solution)/shard_map/pallas_call | solution.py:91
  19.9 6.0 %shard_map.258 = (bf16[64,2304]{1,0:T(8,128)(2,1)S(1)}, bf16[64,2304]{1,0:T(8,128)(2,1)S(1)}, bf16[64,2304]{1,0:T(8,128)(2,1)S(1)}, bf16[64,2304]{1,0:T(8,128)(2...) custom-call(bf16[128,1024]{1,0:T(8,128)(2,1)S(1)} %copy-done.2, ...), custom_call_target="tpu_custom_call" | custom-call | flops 6600000000 | tf_op jit(solution)/shard_map/pallas_call | solution.py:91
  28.3 2.4 %collective-permute-start.11 = (bf16[96,1408]{1,0:T(8,128)(2,1)S(1)}, bf16[96,1408]{1,0:T(8,128)(2,1)S(1)}, u32[]{:S(2)}, u32[]{:S(2)}) collective-permute-start(bf16[96,1408]{1,0:T(8,128)(2,1)S(1)} %collective-permute-done.10.refs_2_), channel_id=1, source_target_pairs={{0,4},{4,0},{8,12},{12,8},{16,20},{20,16},{24,28},{28,24},{1,5},{5... | collective-permute-start | bytes 811016 | tf_op jit(solution)/shard_map/ppermute | solution.py:22
  43.7 11.1 %shard_map.261 = (bf16[64,2048]{1,0:T(8,128)(2,1)S(1)}, bf16[64,2048]{1,0:T(8,128)(2,1)S(1)}, bf16[64,2048]{1,0:T(8,128)(2,1)S(1)}, bf16[64,2048]{1,0:T(8,128)(2...) custom-call(bf16[64,2304]{1,0:T(8,128)(2,1)S(1)} %copy-done.6, ...), custom_call_target="tpu_custom_call" | custom-call | flops 11000000512 | tf_op jit(solution)/shard_map/pallas_call | solution.py:91
  56.3 5.6 %shard_map.262 = (bf16[64,2176]{1,0:T(8,128)(2,1)S(1)}, bf16[64,2176]{1,0:T(8,128)(2,1)S(1)}, bf16[64,2176]{1,0:T(8,128)(2,1)S(1)}, bf16[64,2176]{1,0:T(8,128)(2...) custom-call(bf16[64,2304]{1,0:T(8,128)(2,1)S(1)} %copy-done.4, ...), custom_call_target="tpu_custom_call" | custom-call | flops 11000000512 | tf_op jit(solution)/shard_map/pallas_call | solution.py:91
  62.3 5.4 %shard_map.263 = (bf16[2048,256]{1,0:T(8,128)(2,1)S(1)}, bf16[2048,256]{1,0:T(8,128)(2,1)S(1)}) custom-call(bf16[3,256,2304]{2,1,0:T(8,128)(2,1)S(1)} %get-tuple-element.209.refs_0_, bf16[3,256,2304]{2,1,0:T(8,128)(2,1)S(1)} %get-tuple-element.210.refs_1_, f32[1,2304]{1,0:T(1,128)S(1)} %reshape_reshape.3.refs_5_.refs_6_.refs_2_, ...), custom_call_target="tpu_custom_call" | custom-call | flops 110000000 | tf_op jit(solution)/shard_map/pallas_call | solution.py:91
  67.7 3.1 %collective-permute-done.21.refs_2_ = bf16[64,2176]{1,0:T(8,128)(2,1)S(1)} collective-permute-done((bf16[64,2176]{1,0:T(8,128)(2,1)S(1)}, bf16[64,2176]{1,0:T(8,128)(2,1)S(1)}, u32[]{:S(2)}, u32[]{:S(2)}) %collective-permute-start.21) | collective-permute-done | bytes 278560 | tf_op jit(solution)/shard_map/ppermute | solution.py:22
  73.7 2.5 %collective-permute-start.27 = (bf16[1024,256]{1,0:T(8,128)(2,1)S(1)}, bf16[1024,256]{1,0:T(8,128)(2,1)S(1)}, u32[]{:S(2)}, u32[]{:S(2)}) collective-permute-start(bf16[1024,256]{1,0:T(8,128)(2,1)S(1)} %get-tuple-element.219), channel_id=1, source_target_pairs={{0,4},{4,0},{8,12},{12,8},{16,20},{20,16},{24,28},{28,24},{1,5},{5... | collective-permute-start | bytes 1572872 | tf_op jit(solution)/shard_map/ppermute | solution.py:22
  76.2 3.9 %collective-permute-done.24.refs_3_ = bf16[64,2176]{1,0:T(8,128)(2,1)S(1)} collective-permute-done((bf16[64,2176]{1,0:T(8,128)(2,1)S(1)}, bf16[64,2176]{1,0:T(8,128)(2,1)S(1)}, u32[]{:S(2)}, u32[]{:S(2)}) %collective-permute-start.24) | collective-permute-done | bytes 278560 | tf_op jit(solution)/shard_map/ppermute | solution.py:22
  80.1 5.1 %shard_map.265 = (bf16[1024,1024]{1,0:T(8,128)(2,1)S(1)}, bf16[272,256]{1,0:T(8,128)(2,1)S(1)}, bf16[272,256]{1,0:T(8,128)(2,1)S(1)}, bf16[768,256]{1,0:T(8,128)(2,1)S(1)}, bf16[768,256]{1,0:T(8,128)(2,1)S(1)}) custom-call(bf16[64,2176]{1,0:T(8,128)(2,1)S(1)} %get-tuple-element.224.refs_0_, bf16[64,2176]{1,0:T(8,128)(2,1)S(1)} %collective-permute-done.23.refs_1_, ...), custom_call_target="tpu_custom_call" | custom-call | flops 5500000256 | tf_op jit(solution)/shard_map/pallas_call | solution.py:91
  85.2 2.8 %collective-permute-start.26 = (bf16[768,256]{1,0:T(8,128)(2,1)S(1)}, bf16[768,256]{1,0:T(8,128)(2,1)S(1)}, u32[]{:S(2)}, u32[]{:S(2)}) collective-permute-start(bf16[768,256]{1,0:T(8,128)(2,1)S(1)} %get-tuple-element.239), channel_id=1, source_target_pairs={{0,8},{4,12},{8,0},{12,4},{16,24},{20,28},{24,16},{28,20},{1,9},{5... | collective-permute-start | bytes 1179656 | tf_op jit(solution)/shard_map/ppermute | solution.py:22
  88.0 2.6 %shard_map.266 = (bf16[256,1024]{1,0:T(8,128)(2,1)S(1)}, bf16[256,1024]{1,0:T(8,128)(2,1)S(1)}) custom-call(bf16[1024,512]{1,0:T(8,128)(2,1)} %get-tuple-element.234.refs_0_, bf16[1024,1024]{1,0:T(8,128)(2,1)S(1)} %get-tuple-element.235.refs_1_), custom_call_target="tpu_custom_call" | custom-call | flops 3300000000 | tf_op jit(solution)/shard_map/pallas_call | solution.py:91
  92.9 3.3 %collective-permute-done.25.refs_1_ = bf16[272,256]{1,0:T(8,128)(2,1)S(1)} collective-permute-done((bf16[272,256]{1,0:T(8,128)(2,1)S(1)}, bf16[272,256]{1,0:T(8,128)(2,1)S(1)}, u32[]{:S(2)}, u32[]{:S(2)}) %collective-permute-start.25) | collective-permute-done | bytes 139296 | tf_op jit(solution)/shard_map/ppermute | solution.py:22
  97.6 2.5 %collective-permute-done.28.refs_3_ = bf16[512,256]{1,0:T(8,128)(2,1)S(1)} collective-permute-done((bf16[512,256]{1,0:T(8,128)(2,1)S(1)}, bf16[512,256]{1,0:T(8,128)(2,1)S(1)}, u32[]{:S(2)}, u32[]{:S(2)}) %collective-permute-start.28) | collective-permute-done | bytes 262176 | tf_op jit(solution)/shard_map/ppermute | solution.py:22
  100.8 2.7 %collective-permute-start.30 = (bf16[384,256]{1,0:T(8,128)(2,1)S(1)}, bf16[384,256]{1,0:T(8,128)(2,1)S(1)}, u32[]{:S(2)}, u32[]{:S(2)}) collective-permute-start(bf16[384,256]{1,0:T(8,128)(2,1)S(1)} %get-tuple-element.251), channel_id=1, source_target_pairs={{0,16},{4,20},{8,24},{12,28},{16,0},{20,4},{24,8},{28,12},{1,17},{... | collective-permute-start | bytes 589832 | tf_op jit(solution)/shard_map/ppermute | solution.py:22
  104.5 7.4 %collective-permute-done.30.refs_1_ = bf16[384,256]{1,0:T(8,128)(2,1)S(1)} collective-permute-done((bf16[384,256]{1,0:T(8,128)(2,1)S(1)}, bf16[384,256]{1,0:T(8,128)(2,1)S(1)}, u32[]{:S(2)}, u32[]{:S(2)}) %collective-permute-start.30) | collective-permute-done | bytes 196640 | tf_op jit(solution)/shard_map/ppermute | solution.py:22
  115.6 2.6 %collective-permute-done.32.refs_1_ = bf16[384,256]{1,0:T(8,128)(2,1)S(1)} collective-permute-done((bf16[384,256]{1,0:T(8,128)(2,1)S(1)}, bf16[384,256]{1,0:T(8,128)(2,1)S(1)}, u32[]{:S(2)}, u32[]{:S(2)}) %collective-permute-start.32) | collective-permute-done | bytes 196640 | tf_op jit(solution)/shard_map/ppermute | solution.py:22
  118.1 3.6 %collective-permute-done.31.refs_1_ = bf16[400,256]{1,0:T(8,128)(2,1)S(1)} collective-permute-done((bf16[400,256]{1,0:T(8,128)(2,1)S(1)}, bf16[400,256]{1,0:T(8,128)(2,1)S(1)}, u32[]{:S(2)}, u32[]{:S(2)}) %collective-permute-start.31) | collective-permute-done | bytes 204832 | tf_op jit(solution)/shard_map/ppermute | solution.py:22
  122.0 4.1 %collective-permute-start.35 = (bf16[384,256]{1,0:T(8,128)(2,1)S(1)}, bf16[384,256]{1,0:T(8,128)(2,1)S(1)}, u32[]{:S(2)}, u32[]{:S(2)}) collective-permute-start(bf16[384,256]{1,0:T(8,128)(2,1)S(1)} %get-tuple-element.260.refs_0_), channel_id=1, source_target_pairs={{0,8},{4,12},{8,0},{12,4},{16,24},{20,28},{24,16},{28,20},{1,9},{5... | collective-permute-start | bytes 589832 | tf_op jit(solution)/shard_map/ppermute | solution.py:22
  127.7 3.1 %collective-permute-done.36 = bf16[384,256]{1,0:T(8,128)(2,1)S(1)} collective-permute-done((bf16[384,256]{1,0:T(8,128)(2,1)S(1)}, bf16[384,256]{1,0:T(8,128)(2,1)S(1)}, u32[]{:S(2)}, u32[]{:S(2)}) %collective-permute-start.36) | collective-permute-done | bytes 196640 | tf_op jit(solution)/shard_map/ppermute | solution.py:22
  135.2 2.7 %collective-permute-start.43 = (f32[1,512]{1,0:T(1,128)S(1)}, f32[1,512]{1,0:T(1,128)S(1)}, u32[]{:S(2)}, u32[]{:S(2)}) collective-permute-start(f32[1,512]{1,0:T(1,128)S(1)} %add.35), channel_id=1, source_target_pairs={{0,2},{1,3},{2,0},{3,1},{4,6},{5,7},{6,4},{7,5},{8,10},{9,11},{10,... | collective-permute-start | bytes 6152 | tf_op jit(solution)/shard_map/ppermute | solution.py:22
  142.8 2.9 %shard_map.279 = (f32[16,64,512]{2,1,0:T(8,128)}, f32[1,512]{1,0:T(1,128)}, f32[3,3,64,256]{3,2,1,0:T(8,128)}, f32[3,64]{1,0:T(4,128)}, f32[3,64]{1,0:T(4,128)},...) custom-call(bf16[768,256]{1,0:T(8,128)(2,1)S(1)} %shard_map.277.refs, ...), custom_call_target="tpu_custom_call" | custom-call | flops 5500000256 | tf_op jit(solution)/shard_map/pallas_call | solution.py:91
  (125 shorter events, 50.4 us)
Async XLA Ops:
  0.6 14.1 %collective-permute-start.1 = (bf16[128,1024]{1,0:T(8,128)(2,1)}, bf16[128,1024]{1,0:T(8,128)(2,1)S(1)}, u32[]{:S(2)}, u32[]{:S(2)}) collective-permute-start(bf16[128,1024]{1,0:T(8,128)(2,1)} %refs_2_.2), channel_id=1, source_target_pairs={{0,2},{1,3},{2,0},{3,1},{4,6},{5,7},{6,4},{7,5},{8,10},{9,11},{10,... | collective-permute-start | bytes 786440 | tf_op jit(solution)/shard_map/ppermute | solution.py:22
  27.5 9.9 %collective-permute-start.12 = (bf16[64,2304]{1,0:T(8,128)(2,1)S(1)}, bf16[64,2304]{1,0:T(8,128)(2,1)S(1)}, u32[]{:S(2)}, u32[]{:S(2)}) collective-permute-start(bf16[64,2304]{1,0:T(8,128)(2,1)S(1)} %get-tuple-element.182), channel_id=1, source_target_pairs={{0,2},{1,3},{2,0},{3,1},{4,6},{5,7},{6,4},{7,5},{8,10},{9,11},{10,... | collective-permute-start | bytes 884744 | tf_op jit(solution)/shard_map/ppermute | solution.py:22
  30.7 9.1 %collective-permute-start.13 = (bf16[192,1408]{1,0:T(8,128)(2,1)S(1)}, bf16[192,1408]{1,0:T(8,128)(2,1)S(1)}, u32[]{:S(2)}, u32[]{:S(2)}) collective-permute-start(bf16[192,1408]{1,0:T(8,128)(2,1)S(1)} %get-tuple-element.192.refs_0_), channel_id=1, source_target_pairs={{0,1},{1,0},{2,3},{3,2},{4,5},{5,4},{6,7},{7,6},{8,9},{9,8},{10,11... | collective-permute-start | bytes 1622024 | tf_op jit(solution)/shard_map/ppermute | solution.py:22
  30.7 12.0 %collective-permute-start.19 = (bf16[64,2304]{1,0:T(8,128)(2,1)S(1)}, bf16[64,2304]{1,0:T(8,128)(2,1)}, u32[]{:S(2)}, u32[]{:S(2)}) collective-permute-start(bf16[64,2304]{1,0:T(8,128)(2,1)S(1)} %get-tuple-element.203), channel_id=1, source_target_pairs={{0,1},{1,0},{2,3},{3,2},{4,5},{5,4},{6,7},{7,6},{8,9},{9,8},{10,11... | collective-permute-start | bytes 884744 | tf_op jit(solution)/shard_map/ppermute | solution.py:22
  31.2 11.5 %collective-permute-start.20 = (bf16[64,2304]{1,0:T(8,128)(2,1)S(1)}, bf16[64,2304]{1,0:T(8,128)(2,1)}, u32[]{:S(2)}, u32[]{:S(2)}) collective-permute-start(bf16[64,2304]{1,0:T(8,128)(2,1)S(1)} %get-tuple-element.205), channel_id=1, source_target_pairs={{0,3},{1,2},{2,1},{3,0},{4,7},{5,6},{6,5},{7,4},{8,11},{9,10},{10,... | collective-permute-start | bytes 884744 | tf_op jit(solution)/shard_map/ppermute | solution.py:22
  40.8 14.0 %collective-permute-start.16 = (bf16[64,2304]{1,0:T(8,128)(2,1)}, bf16[64,2304]{1,0:T(8,128)(2,1)S(1)}, u32[]{:S(2)}, u32[]{:S(2)}) collective-permute-start(bf16[64,2304]{1,0:T(8,128)(2,1)} %copy-done.1), channel_id=1, source_target_pairs={{0,1},{1,0},{2,3},{3,2},{4,5},{5,4},{6,7},{7,6},{8,9},{9,8},{10,11... | collective-permute-start | bytes 884744 | tf_op jit(solution)/shard_map/ppermute | solution.py:22
  40.8 14.0 %collective-permute-start.17 = (bf16[64,2304]{1,0:T(8,128)(2,1)}, bf16[64,2304]{1,0:T(8,128)(2,1)S(1)}, u32[]{:S(2)}, u32[]{:S(2)}) collective-permute-start(bf16[64,2304]{1,0:T(8,128)(2,1)} %copy-done), channel_id=1, source_target_pairs={{0,2},{1,3},{2,0},{3,1},{4,6},{5,7},{6,4},{7,5},{8,10},{9,11},{10,... | collective-permute-start | bytes 884744 | tf_op jit(solution)/shard_map/ppermute | solution.py:22
  41.3 15.1 %collective-permute-start.18 = (bf16[64,2304]{1,0:T(8,128)(2,1)S(1)}, bf16[64,2304]{1,0:T(8,128)(2,1)S(1)}, u32[]{:S(2)}, u32[]{:S(2)}) collective-permute-start(bf16[64,2304]{1,0:T(8,128)(2,1)S(1)} %get-tuple-element.199), channel_id=1, source_target_pairs={{0,3},{1,2},{2,1},{3,0},{4,7},{5,6},{6,5},{7,4},{8,11},{9,10},{10,... | collective-permute-start | bytes 884744 | tf_op jit(solution)/shard_map/ppermute | solution.py:22
  61.9 8.9 %collective-permute-start.21 = (bf16[64,2176]{1,0:T(8,128)(2,1)S(1)}, bf16[64,2176]{1,0:T(8,128)(2,1)S(1)}, u32[]{:S(2)}, u32[]{:S(2)}) collective-permute-start(bf16[64,2176]{1,0:T(8,128)(2,1)S(1)} %get-tuple-element.216), channel_id=1, source_target_pairs={{0,2},{1,3},{2,0},{3,1},{4,6},{5,7},{6,4},{7,5},{8,10},{9,11},{10,... | collective-permute-start | bytes 835592 | tf_op jit(solution)/shard_map/ppermute | solution.py:22
  71.3 8.8 %collective-permute-start.24 = (bf16[64,2176]{1,0:T(8,128)(2,1)S(1)}, bf16[64,2176]{1,0:T(8,128)(2,1)S(1)}, u32[]{:S(2)}, u32[]{:S(2)}) collective-permute-start(bf16[64,2176]{1,0:T(8,128)(2,1)S(1)} %get-tuple-element.223), channel_id=1, source_target_pairs={{0,3},{1,2},{2,1},{3,0},{4,7},{5,6},{6,5},{7,4},{8,11},{9,10},{10,... | collective-permute-start | bytes 835592 | tf_op jit(solution)/shard_map/ppermute | solution.py:22
  73.7 18.2 %collective-permute-start.27 = (bf16[1024,256]{1,0:T(8,128)(2,1)S(1)}, bf16[1024,256]{1,0:T(8,128)(2,1)S(1)}, u32[]{:S(2)}, u32[]{:S(2)}) collective-permute-start(bf16[1024,256]{1,0:T(8,128)(2,1)S(1)} %get-tuple-element.219), channel_id=1, source_target_pairs={{0,4},{4,0},{8,12},{12,8},{16,20},{20,16},{24,28},{28,24},{1,5},{5... | collective-permute-start | bytes 1572872 | tf_op jit(solution)/shard_map/ppermute | solution.py:22
  85.2 12.4 %collective-permute-start.26 = (bf16[768,256]{1,0:T(8,128)(2,1)S(1)}, bf16[768,256]{1,0:T(8,128)(2,1)S(1)}, u32[]{:S(2)}, u32[]{:S(2)}) collective-permute-start(bf16[768,256]{1,0:T(8,128)(2,1)S(1)} %get-tuple-element.239), channel_id=1, source_target_pairs={{0,8},{4,12},{8,0},{12,4},{16,24},{20,28},{24,16},{28,20},{1,9},{5... | collective-permute-start | bytes 1179656 | tf_op jit(solution)/shard_map/ppermute | solution.py:22
  100.2 11.7 %collective-permute-start.29 = (bf16[400,256]{1,0:T(8,128)(2,1)S(1)}, bf16[400,256]{1,0:T(8,128)(2,1)S(1)}, u32[]{:S(2)}, u32[]{:S(2)}) collective-permute-start(bf16[400,256]{1,0:T(8,128)(2,1)S(1)} %get-tuple-element.248), channel_id=1, source_target_pairs={{0,8},{4,12},{8,0},{12,4},{16,24},{20,28},{24,16},{28,20},{1,9},{5... | collective-permute-start | bytes 614408 | tf_op jit(solution)/shard_map/ppermute | solution.py:22
  100.8 11.1 %collective-permute-start.30 = (bf16[384,256]{1,0:T(8,128)(2,1)S(1)}, bf16[384,256]{1,0:T(8,128)(2,1)S(1)}, u32[]{:S(2)}, u32[]{:S(2)}) collective-permute-start(bf16[384,256]{1,0:T(8,128)(2,1)S(1)} %get-tuple-element.251), channel_id=1, source_target_pairs={{0,16},{4,20},{8,24},{12,28},{16,0},{20,4},{24,8},{28,12},{1,17},{... | collective-permute-start | bytes 589832 | tf_op jit(solution)/shard_map/ppermute | solution.py:22
  103.6 10.9 %collective-permute-start.34 = (bf16[128,1024]{1,0:T(8,128)(2,1)S(1)}, bf16[128,1024]{1,0:T(8,128)(2,1)S(1)}, u32[]{:S(2)}, u32[]{:S(2)}) collective-permute-start(bf16[128,1024]{1,0:T(8,128)(2,1)S(1)} %get-tuple-element.258), channel_id=1, source_target_pairs={{0,2},{1,3},{2,0},{3,1},{4,6},{5,7},{6,4},{7,5},{8,10},{9,11},{10,... | collective-permute-start | bytes 786440 | tf_op jit(solution)/shard_map/ppermute | solution.py:22
  111.9 9.8 %collective-permute-start.31 = (bf16[400,256]{1,0:T(8,128)(2,1)S(1)}, bf16[400,256]{1,0:T(8,128)(2,1)S(1)}, u32[]{:S(2)}, u32[]{:S(2)}) collective-permute-start(bf16[400,256]{1,0:T(8,128)(2,1)S(1)} %shard_map.270.refs_0_), channel_id=1, source_target_pairs={{0,16},{4,20},{8,24},{12,28},{16,0},{20,4},{24,8},{28,12},{1,17},{... | collective-permute-start | bytes 614408 | tf_op jit(solution)/shard_map/ppermute | solution.py:22
  113.7 12.9 %collective-permute-start.37 = (bf16[64,2048]{1,0:T(8,128)(2,1)S(1)}, bf16[64,2048]{1,0:T(8,128)(2,1)S(1)}, u32[]{:S(2)}, u32[]{:S(2)}) collective-permute-start(bf16[64,2048]{1,0:T(8,128)(2,1)S(1)} %get-tuple-element.263), channel_id=1, source_target_pairs={{0,1},{1,0},{2,3},{3,2},{4,5},{5,4},{6,7},{7,6},{8,9},{9,8},{10,11... | collective-permute-start | bytes 786440 | tf_op jit(solution)/shard_map/ppermute | solution.py:22
  113.7 12.9 %collective-permute-start.38 = (bf16[64,2048]{1,0:T(8,128)(2,1)S(1)}, bf16[64,2048]{1,0:T(8,128)(2,1)S(1)}, u32[]{:S(2)}, u32[]{:S(2)}) collective-permute-start(bf16[64,2048]{1,0:T(8,128)(2,1)S(1)} %get-tuple-element.264), channel_id=1, source_target_pairs={{0,2},{1,3},{2,0},{3,1},{4,6},{5,7},{6,4},{7,5},{8,10},{9,11},{10,... | collective-permute-start | bytes 786440 | tf_op jit(solution)/shard_map/ppermute | solution.py:22
  114.5 13.1 %collective-permute-start.39 = (bf16[64,2048]{1,0:T(8,128)(2,1)S(1)}, bf16[64,2048]{1,0:T(8,128)(2,1)S(1)}, u32[]{:S(2)}, u32[]{:S(2)}) collective-permute-start(bf16[64,2048]{1,0:T(8,128)(2,1)S(1)} %get-tuple-element.265), channel_id=1, source_target_pairs={{0,3},{1,2},{2,1},{3,0},{4,7},{5,6},{6,5},{7,4},{8,11},{9,10},{10,... | collective-permute-start | bytes 786440 | tf_op jit(solution)/shard_map/ppermute | solution.py:22
  121.9 8.8 %collective-permute-start.36 = (bf16[384,256]{1,0:T(8,128)(2,1)S(1)}, bf16[384,256]{1,0:T(8,128)(2,1)S(1)}, u32[]{:S(2)}, u32[]{:S(2)}) collective-permute-start(bf16[384,256]{1,0:T(8,128)(2,1)S(1)} %shard_map.274), channel_id=1, source_target_pairs={{0,16},{4,20},{8,24},{12,28},{16,0},{20,4},{24,8},{28,12},{1,17},{... | collective-permute-start | bytes 589832 | tf_op jit(solution)/shard_map/ppermute | solution.py:22
  122.0 8.9 %collective-permute-start.35 = (bf16[384,256]{1,0:T(8,128)(2,1)S(1)}, bf16[384,256]{1,0:T(8,128)(2,1)S(1)}, u32[]{:S(2)}, u32[]{:S(2)}) collective-permute-start(bf16[384,256]{1,0:T(8,128)(2,1)S(1)} %get-tuple-element.260.refs_0_), channel_id=1, source_target_pairs={{0,8},{4,12},{8,0},{12,4},{16,24},{20,28},{24,16},{28,20},{1,9},{5... | collective-permute-start | bytes 589832 | tf_op jit(solution)/shard_map/ppermute | solution.py:22
  126.6 8.6 %collective-permute-start.42 = (f32[1,512]{1,0:T(1,128)S(1)}, f32[1,512]{1,0:T(1,128)S(1)}, u32[]{:S(2)}, u32[]{:S(2)}) collective-permute-start(f32[1,512]{1,0:T(1,128)S(1)} %bitcast.10), channel_id=1, source_target_pairs={{0,1},{1,0},{2,3},{3,2},{4,5},{5,4},{6,7},{7,6},{8,9},{9,8},{10,11... | collective-permute-start | bytes 6152 | tf_op jit(solution)/shard_map/ppermute | solution.py:22
  130.9 10.4 %collective-permute-start.41 = (bf16[768,256]{1,0:T(8,128)(2,1)S(1)}, bf16[768,256]{1,0:T(8,128)(2,1)S(1)}, u32[]{:S(2)}, u32[]{:S(2)}) collective-permute-start(bf16[768,256]{1,0:T(8,128)(2,1)S(1)} %pad_maximum_fusion.refs_2_), channel_id=1, source_target_pairs={{0,8},{4,12},{8,0},{12,4},{16,24},{20,28},{24,16},{28,20},{1,9},{5... | collective-permute-start | bytes 1179656 | tf_op jit(solution)/shard_map/ppermute | solution.py:22
  131.9 10.9 %collective-permute-start.40 = (bf16[768,256]{1,0:T(8,128)(2,1)S(1)}, bf16[768,256]{1,0:T(8,128)(2,1)S(1)}, u32[]{:S(2)}, u32[]{:S(2)}) collective-permute-start(bf16[768,256]{1,0:T(8,128)(2,1)S(1)} %shard_map.277.refs_0_), channel_id=1, source_target_pairs={{0,4},{4,0},{8,12},{12,8},{16,20},{20,16},{24,28},{28,24},{1,5},{5... | collective-permute-start | bytes 1179656 | tf_op jit(solution)/shard_map/ppermute | solution.py:22
  (28 other events, 129.1 us)

commit v2 on v1

--- a/solution.py
+++ b/solution.py
@@ -904,7 +904,7 @@
         [cotangent, silence_row, low_edge, high_edge],
         "FFVV",
         scratch=[pltpu.VMEM((rows, length + 2 * HALO), BF)],
-        micros=2,
+        micros=0.05,
     )
     all_hidden = exchange_chan(hidden_parts)
     all_packed = [packed, swap(packed, "chan", 1)]
@@ -922,7 +922,7 @@
         ],
         all_packed,
         "V" * len(all_packed),
-        micros=0.1,
+        micros=0.001,
     )
     cut, plain = tie((list(cut), plain))
     all_err = exchange_chan(cut)

time: 146 us -> 146 us (level)
    unnamed x18 -> x16, local copies, waits for them, and re-layouts: 3.84 us -> 3.85 us
where the time goes in v2:
time: 146 us
  Pallas kernels  52.1 us (36%)
  starting transfers between devices  43.1 us (30%)
  waiting for transfers between devices  43 us (29%)
  local copies, waits for them, and re-layouts  6.37 us (4%)
    pallas_call x25, Pallas kernels, kernel_call(): pl.pallas_call(wrapped, out_shape=tuple(out_shape), in_specs=in_specs, ou...  52.1 us
    ppermute x42, waiting for transfers between devices, swap(): return lax.ppermute(values, axis, [(k, k ^ bit) for k in range(count)])  41.9 us
    ppermute x42, starting transfers between devices, swap(): return lax.ppermute(values, axis, [(k, k ^ bit) for k in range(count)])  38.2 us
    unnamed x16, local copies, waits for them, and re-layouts  3.85 us
    ppermute x1, starting transfers between devices, local(): low_edge = lax.ppermute(ahead, 'tm', forward)  3.43 us
  transfers between devices with their start and end apart: 44, of which 22 were waited for; matrix products, arithmetic and copies ran while one was open for 2% of the time, Pallas kernels for 30%

profile of v2, /device:TPU:0, one launch (start us, length us, event | category | flops | bytes accessed | tf_op | source)
XLA Modules:
  0.0 145.8 jit_solution(6299532764754079735)
XLA Ops:
  0.6 3.0 %collective-permute-start.1 = (bf16[128,1024]{1,0:T(8,128)(2,1)}, bf16[128,1024]{1,0:T(8,128)(2,1)S(1)}, u32[]{:S(2)}, u32[]{:S(2)}) collective-permute-start(bf16[128,1024]{1,0:T(8,128)(2,1)} %refs_2_.2), channel_id=1, source_target_pairs={{0,2},{1,3},{2,0},{3,1},{4,6},{5,7},{6,4},{7,5},{8,10},{9,11},{10,... | collective-permute-start | bytes 786440 | tf_op jit(solution)/shard_map/ppermute | solution.py:22
  4.5 3.4 %collective-permute-start.3 = (bf16[192,128]{1,0:T(8,128)(2,1)S(1)}, bf16[192,128]{1,0:T(8,128)(2,1)S(1)}, u32[]{:S(2)}, u32[]{:S(2)}) collective-permute-start(bf16[192,128]{1,0:T(8,128)(2,1)S(1)} %get-tuple-element.157), channel_id=1, source_target_pairs={{0,4},{4,8},{8,12},{12,16},{16,20},{20,24},{24,28},{1,5},{5,9},{9,... | collective-permute-start | bytes 147464 | tf_op jit(solution)/shard_map/ppermute | solution.py:819
  14.7 2.4 %shard_map.256 = (bf16[192,1408]{1,0:T(8,128)(2,1)S(1)}, bf16[96,1408]{1,0:T(8,128)(2,1)S(1)}, bf16[96,1408]{1,0:T(8,128)(2,1)}, f32[1,512]{1,0:T(1,128)S(1)}, f32[1,64]{1,0:T(1,128)S(1)}) custom-call(f32[3,3,64,256]{3,2,1,0:T(8,128)} %refs_1_.3, f32[3,64]{1,0:T(4,128)} %refs_2_.3, f32[3,64]{1,0:T(4,128)} %refs_2_.1, f32[3,64,256]{2,1,0:T(8,128)} %refs_3_.1, ...), custom_call_target="tpu_custom_call" | custom-call | flops 3300000000 | tf_op jit(solution)/shard_map/pallas_call | solution.py:91
  19.9 6.0 %shard_map.258 = (bf16[64,2304]{1,0:T(8,128)(2,1)S(1)}, bf16[64,2304]{1,0:T(8,128)(2,1)S(1)}, bf16[64,2304]{1,0:T(8,128)(2,1)S(1)}, bf16[64,2304]{1,0:T(8,128)(2...) custom-call(bf16[128,1024]{1,0:T(8,128)(2,1)S(1)} %copy-done.3, ...), custom_call_target="tpu_custom_call" | custom-call | flops 6600000000 | tf_op jit(solution)/shard_map/pallas_call | solution.py:91
  28.3 2.4 %collective-permute-start.11 = (bf16[96,1408]{1,0:T(8,128)(2,1)S(1)}, bf16[96,1408]{1,0:T(8,128)(2,1)S(1)}, u32[]{:S(2)}, u32[]{:S(2)}) collective-permute-start(bf16[96,1408]{1,0:T(8,128)(2,1)S(1)} %collective-permute-done.10.refs_2_), channel_id=1, source_target_pairs={{0,4},{4,0},{8,12},{12,8},{16,20},{20,16},{24,28},{28,24},{1,5},{5... | collective-permute-start | bytes 811016 | tf_op jit(solution)/shard_map/ppermute | solution.py:22
  43.7 11.1 %shard_map.261 = (bf16[64,2048]{1,0:T(8,128)(2,1)S(1)}, bf16[64,2048]{1,0:T(8,128)(2,1)S(1)}, bf16[64,2048]{1,0:T(8,128)(2,1)S(1)}, bf16[64,2048]{1,0:T(8,128)(2...) custom-call(bf16[64,2304]{1,0:T(8,128)(2,1)S(1)} %copy-done.5, ...), custom_call_target="tpu_custom_call" | custom-call | flops 11000000512 | tf_op jit(solution)/shard_map/pallas_call | solution.py:91
  56.3 5.6 %shard_map.262 = (bf16[64,2176]{1,0:T(8,128)(2,1)S(1)}, bf16[64,2176]{1,0:T(8,128)(2,1)S(1)}, bf16[64,2176]{1,0:T(8,128)(2,1)S(1)}, bf16[64,2176]{1,0:T(8,128)(2...) custom-call(bf16[64,2304]{1,0:T(8,128)(2,1)S(1)} %get-tuple-element.196.refs_0_, ...), custom_call_target="tpu_custom_call" | custom-call | flops 11000000512 | tf_op jit(solution)/shard_map/pallas_call | solution.py:91
  62.3 5.4 %shard_map.263 = (bf16[2048,256]{1,0:T(8,128)(2,1)S(1)}, bf16[2048,256]{1,0:T(8,128)(2,1)S(1)}) custom-call(bf16[3,256,2304]{2,1,0:T(8,128)(2,1)S(1)} %get-tuple-element.209.refs_0_, bf16[3,256,2304]{2,1,0:T(8,128)(2,1)S(1)} %get-tuple-element.210.refs_1_, f32[1,2304]{1,0:T(1,128)S(1)} %reshape_reshape.3.refs_5_.refs_6_.refs_2_, ...), custom_call_target="tpu_custom_call" | custom-call | flops 110000000 | tf_op jit(solution)/shard_map/pallas_call | solution.py:91
  67.7 3.1 %collective-permute-done.21.refs_2_ = bf16[64,2176]{1,0:T(8,128)(2,1)S(1)} collective-permute-done((bf16[64,2176]{1,0:T(8,128)(2,1)S(1)}, bf16[64,2176]{1,0:T(8,128)(2,1)S(1)}, u32[]{:S(2)}, u32[]{:S(2)}) %collective-permute-start.21) | collective-permute-done | bytes 278560 | tf_op jit(solution)/shard_map/ppermute | solution.py:22
  73.7 2.5 %collective-permute-start.27 = (bf16[1024,256]{1,0:T(8,128)(2,1)S(1)}, bf16[1024,256]{1,0:T(8,128)(2,1)S(1)}, u32[]{:S(2)}, u32[]{:S(2)}) collective-permute-start(bf16[1024,256]{1,0:T(8,128)(2,1)S(1)} %get-tuple-element.219), channel_id=1, source_target_pairs={{0,4},{4,0},{8,12},{12,8},{16,20},{20,16},{24,28},{28,24},{1,5},{5... | collective-permute-start | bytes 1572872 | tf_op jit(solution)/shard_map/ppermute | solution.py:22
  76.2 3.9 %collective-permute-done.24.refs_3_ = bf16[64,2176]{1,0:T(8,128)(2,1)S(1)} collective-permute-done((bf16[64,2176]{1,0:T(8,128)(2,1)S(1)}, bf16[64,2176]{1,0:T(8,128)(2,1)S(1)}, u32[]{:S(2)}, u32[]{:S(2)}) %collective-permute-start.24) | collective-permute-done | bytes 278560 | tf_op jit(solution)/shard_map/ppermute | solution.py:22
  80.1 5.1 %shard_map.265 = (bf16[1024,1024]{1,0:T(8,128)(2,1)S(1)}, bf16[272,256]{1,0:T(8,128)(2,1)S(1)}, bf16[272,256]{1,0:T(8,128)(2,1)S(1)}, bf16[768,256]{1,0:T(8,128)(2,1)S(1)}, bf16[768,256]{1,0:T(8,128)(2,1)S(1)}) custom-call(bf16[64,2176]{1,0:T(8,128)(2,1)S(1)} %get-tuple-element.224.refs_0_, bf16[64,2176]{1,0:T(8,128)(2,1)S(1)} %collective-permute-done.23.refs_1_, ...), custom_call_target="tpu_custom_call" | custom-call | flops 5500000256 | tf_op jit(solution)/shard_map/pallas_call | solution.py:91
  85.2 2.8 %collective-permute-start.26 = (bf16[768,256]{1,0:T(8,128)(2,1)S(1)}, bf16[768,256]{1,0:T(8,128)(2,1)S(1)}, u32[]{:S(2)}, u32[]{:S(2)}) collective-permute-start(bf16[768,256]{1,0:T(8,128)(2,1)S(1)} %get-tuple-element.239), channel_id=1, source_target_pairs={{0,8},{4,12},{8,0},{12,4},{16,24},{20,28},{24,16},{28,20},{1,9},{5... | collective-permute-start | bytes 1179656 | tf_op jit(solution)/shard_map/ppermute | solution.py:22
  88.0 2.6 %shard_map.266 = (bf16[256,1024]{1,0:T(8,128)(2,1)S(1)}, bf16[256,1024]{1,0:T(8,128)(2,1)S(1)}) custom-call(bf16[1024,512]{1,0:T(8,128)(2,1)} %get-tuple-element.234.refs_0_, bf16[1024,1024]{1,0:T(8,128)(2,1)S(1)} %get-tuple-element.235.refs_1_), custom_call_target="tpu_custom_call" | custom-call | flops 3300000000 | tf_op jit(solution)/shard_map/pallas_call | solution.py:91
  92.9 3.4 %collective-permute-done.25.refs_1_ = bf16[272,256]{1,0:T(8,128)(2,1)S(1)} collective-permute-done((bf16[272,256]{1,0:T(8,128)(2,1)S(1)}, bf16[272,256]{1,0:T(8,128)(2,1)S(1)}, u32[]{:S(2)}, u32[]{:S(2)}) %collective-permute-start.25) | collective-permute-done | bytes 139296 | tf_op jit(solution)/shard_map/ppermute | solution.py:22
  97.6 2.5 %collective-permute-done.28.refs_3_ = bf16[512,256]{1,0:T(8,128)(2,1)S(1)} collective-permute-done((bf16[512,256]{1,0:T(8,128)(2,1)S(1)}, bf16[512,256]{1,0:T(8,128)(2,1)S(1)}, u32[]{:S(2)}, u32[]{:S(2)}) %collective-permute-start.28) | collective-permute-done | bytes 262176 | tf_op jit(solution)/shard_map/ppermute | solution.py:22
  100.8 2.7 %collective-permute-start.30 = (bf16[384,256]{1,0:T(8,128)(2,1)S(1)}, bf16[384,256]{1,0:T(8,128)(2,1)S(1)}, u32[]{:S(2)}, u32[]{:S(2)}) collective-permute-start(bf16[384,256]{1,0:T(8,128)(2,1)S(1)} %get-tuple-element.251), channel_id=1, source_target_pairs={{0,16},{4,20},{8,24},{12,28},{16,0},{20,4},{24,8},{28,12},{1,17},{... | collective-permute-start | bytes 589832 | tf_op jit(solution)/shard_map/ppermute | solution.py:22
  104.4 7.4 %collective-permute-done.30.refs_1_ = bf16[384,256]{1,0:T(8,128)(2,1)S(1)} collective-permute-done((bf16[384,256]{1,0:T(8,128)(2,1)S(1)}, bf16[384,256]{1,0:T(8,128)(2,1)S(1)}, u32[]{:S(2)}, u32[]{:S(2)}) %collective-permute-start.30) | collective-permute-done | bytes 196640 | tf_op jit(solution)/shard_map/ppermute | solution.py:22
  115.5 2.6 %collective-permute-done.32.refs_1_ = bf16[384,256]{1,0:T(8,128)(2,1)S(1)} collective-permute-done((bf16[384,256]{1,0:T(8,128)(2,1)S(1)}, bf16[384,256]{1,0:T(8,128)(2,1)S(1)}, u32[]{:S(2)}, u32[]{:S(2)}) %collective-permute-start.32) | collective-permute-done | bytes 196640 | tf_op jit(solution)/shard_map/ppermute | solution.py:22
  118.1 3.6 %collective-permute-done.31.refs_1_ = bf16[400,256]{1,0:T(8,128)(2,1)S(1)} collective-permute-done((bf16[400,256]{1,0:T(8,128)(2,1)S(1)}, bf16[400,256]{1,0:T(8,128)(2,1)S(1)}, u32[]{:S(2)}, u32[]{:S(2)}) %collective-permute-start.31) | collective-permute-done | bytes 204832 | tf_op jit(solution)/shard_map/ppermute | solution.py:22
  121.9 4.2 %collective-permute-start.35 = (bf16[384,256]{1,0:T(8,128)(2,1)S(1)}, bf16[384,256]{1,0:T(8,128)(2,1)S(1)}, u32[]{:S(2)}, u32[]{:S(2)}) collective-permute-start(bf16[384,256]{1,0:T(8,128)(2,1)S(1)} %get-tuple-element.260.refs_0_), channel_id=1, source_target_pairs={{0,8},{4,12},{8,0},{12,4},{16,24},{20,28},{24,16},{28,20},{1,9},{5... | collective-permute-start | bytes 589832 | tf_op jit(solution)/shard_map/ppermute | solution.py:22
  127.6 3.1 %collective-permute-done.36 = bf16[384,256]{1,0:T(8,128)(2,1)S(1)} collective-permute-done((bf16[384,256]{1,0:T(8,128)(2,1)S(1)}, bf16[384,256]{1,0:T(8,128)(2,1)S(1)}, u32[]{:S(2)}, u32[]{:S(2)}) %collective-permute-start.36) | collective-permute-done | bytes 196640 | tf_op jit(solution)/shard_map/ppermute | solution.py:22
  135.2 2.7 %collective-permute-start.43 = (f32[1,512]{1,0:T(1,128)S(1)}, f32[1,512]{1,0:T(1,128)S(1)}, u32[]{:S(2)}, u32[]{:S(2)}) collective-permute-start(f32[1,512]{1,0:T(1,128)S(1)} %add.35), channel_id=1, source_target_pairs={{0,2},{1,3},{2,0},{3,1},{4,6},{5,7},{6,4},{7,5},{8,10},{9,11},{10,... | collective-permute-start | bytes 6152 | tf_op jit(solution)/shard_map/ppermute | solution.py:22
  142.7 2.9 %shard_map.279 = (f32[16,64,512]{2,1,0:T(8,128)}, f32[1,512]{1,0:T(1,128)}, f32[3,3,64,256]{3,2,1,0:T(8,128)}, f32[3,64]{1,0:T(4,128)}, f32[3,64]{1,0:T(4,128)},...) custom-call(bf16[768,256]{1,0:T(8,128)(2,1)S(1)} %shard_map.277.refs, ...), custom_call_target="tpu_custom_call" | custom-call | flops 5500000256 | tf_op jit(solution)/shard_map/pallas_call | solution.py:91
  (123 shorter events, 50.4 us)
Async XLA Ops:
  0.6 14.1 %collective-permute-start.1 = (bf16[128,1024]{1,0:T(8,128)(2,1)}, bf16[128,1024]{1,0:T(8,128)(2,1)S(1)}, u32[]{:S(2)}, u32[]{:S(2)}) collective-permute-start(bf16[128,1024]{1,0:T(8,128)(2,1)} %refs_2_.2), channel_id=1, source_target_pairs={{0,2},{1,3},{2,0},{3,1},{4,6},{5,7},{6,4},{7,5},{8,10},{9,11},{10,... | collective-permute-start | bytes 786440 | tf_op jit(solution)/shard_map/ppermute | solution.py:22
  27.5 9.9 %collective-permute-start.12 = (bf16[64,2304]{1,0:T(8,128)(2,1)S(1)}, bf16[64,2304]{1,0:T(8,128)(2,1)S(1)}, u32[]{:S(2)}, u32[]{:S(2)}) collective-permute-start(bf16[64,2304]{1,0:T(8,128)(2,1)S(1)} %get-tuple-element.182), channel_id=1, source_target_pairs={{0,2},{1,3},{2,0},{3,1},{4,6},{5,7},{6,4},{7,5},{8,10},{9,11},{10,... | collective-permute-start | bytes 884744 | tf_op jit(solution)/shard_map/ppermute | solution.py:22
  30.7 9.1 %collective-permute-start.13 = (bf16[192,1408]{1,0:T(8,128)(2,1)S(1)}, bf16[192,1408]{1,0:T(8,128)(2,1)S(1)}, u32[]{:S(2)}, u32[]{:S(2)}) collective-permute-start(bf16[192,1408]{1,0:T(8,128)(2,1)S(1)} %get-tuple-element.192.refs_0_), channel_id=1, source_target_pairs={{0,1},{1,0},{2,3},{3,2},{4,5},{5,4},{6,7},{7,6},{8,9},{9,8},{10,11... | collective-permute-start | bytes 1622024 | tf_op jit(solution)/shard_map/ppermute | solution.py:22
  30.7 12.0 %collective-permute-start.19 = (bf16[64,2304]{1,0:T(8,128)(2,1)S(1)}, bf16[64,2304]{1,0:T(8,128)(2,1)}, u32[]{:S(2)}, u32[]{:S(2)}) collective-permute-start(bf16[64,2304]{1,0:T(8,128)(2,1)S(1)} %get-tuple-element.203), channel_id=1, source_target_pairs={{0,1},{1,0},{2,3},{3,2},{4,5},{5,4},{6,7},{7,6},{8,9},{9,8},{10,11... | collective-permute-start | bytes 884744 | tf_op jit(solution)/shard_map/ppermute | solution.py:22
  31.2 11.5 %collective-permute-start.20 = (bf16[64,2304]{1,0:T(8,128)(2,1)S(1)}, bf16[64,2304]{1,0:T(8,128)(2,1)}, u32[]{:S(2)}, u32[]{:S(2)}) collective-permute-start(bf16[64,2304]{1,0:T(8,128)(2,1)S(1)} %get-tuple-element.205), channel_id=1, source_target_pairs={{0,3},{1,2},{2,1},{3,0},{4,7},{5,6},{6,5},{7,4},{8,11},{9,10},{10,... | collective-permute-start | bytes 884744 | tf_op jit(solution)/shard_map/ppermute | solution.py:22
  40.8 14.0 %collective-permute-start.16 = (bf16[64,2304]{1,0:T(8,128)(2,1)}, bf16[64,2304]{1,0:T(8,128)(2,1)S(1)}, u32[]{:S(2)}, u32[]{:S(2)}) collective-permute-start(bf16[64,2304]{1,0:T(8,128)(2,1)} %copy-done.2), channel_id=1, source_target_pairs={{0,1},{1,0},{2,3},{3,2},{4,5},{5,4},{6,7},{7,6},{8,9},{9,8},{10,11... | collective-permute-start | bytes 884744 | tf_op jit(solution)/shard_map/ppermute | solution.py:22
  40.8 13.9 %collective-permute-start.17 = (bf16[64,2304]{1,0:T(8,128)(2,1)}, bf16[64,2304]{1,0:T(8,128)(2,1)S(1)}, u32[]{:S(2)}, u32[]{:S(2)}) collective-permute-start(bf16[64,2304]{1,0:T(8,128)(2,1)} %copy-done.1), channel_id=1, source_target_pairs={{0,2},{1,3},{2,0},{3,1},{4,6},{5,7},{6,4},{7,5},{8,10},{9,11},{10,... | collective-permute-start | bytes 884744 | tf_op jit(solution)/shard_map/ppermute | solution.py:22
  41.2 15.1 %collective-permute-start.18 = (bf16[64,2304]{1,0:T(8,128)(2,1)}, bf16[64,2304]{1,0:T(8,128)(2,1)S(1)}, u32[]{:S(2)}, u32[]{:S(2)}) collective-permute-start(bf16[64,2304]{1,0:T(8,128)(2,1)} %copy-done), channel_id=1, source_target_pairs={{0,3},{1,2},{2,1},{3,0},{4,7},{5,6},{6,5},{7,4},{8,11},{9,10},{10,... | collective-permute-start | bytes 884744 | tf_op jit(solution)/shard_map/ppermute | solution.py:22
  61.9 8.9 %collective-permute-start.21 = (bf16[64,2176]{1,0:T(8,128)(2,1)S(1)}, bf16[64,2176]{1,0:T(8,128)(2,1)S(1)}, u32[]{:S(2)}, u32[]{:S(2)}) collective-permute-start(bf16[64,2176]{1,0:T(8,128)(2,1)S(1)} %get-tuple-element.216), channel_id=1, source_target_pairs={{0,2},{1,3},{2,0},{3,1},{4,6},{5,7},{6,4},{7,5},{8,10},{9,11},{10,... | collective-permute-start | bytes 835592 | tf_op jit(solution)/shard_map/ppermute | solution.py:22
  71.3 8.8 %collective-permute-start.24 = (bf16[64,2176]{1,0:T(8,128)(2,1)S(1)}, bf16[64,2176]{1,0:T(8,128)(2,1)S(1)}, u32[]{:S(2)}, u32[]{:S(2)}) collective-permute-start(bf16[64,2176]{1,0:T(8,128)(2,1)S(1)} %get-tuple-element.223), channel_id=1, source_target_pairs={{0,3},{1,2},{2,1},{3,0},{4,7},{5,6},{6,5},{7,4},{8,11},{9,10},{10,... | collective-permute-start | bytes 835592 | tf_op jit(solution)/shard_map/ppermute | solution.py:22
  73.7 18.2 %collective-permute-start.27 = (bf16[1024,256]{1,0:T(8,128)(2,1)S(1)}, bf16[1024,256]{1,0:T(8,128)(2,1)S(1)}, u32[]{:S(2)}, u32[]{:S(2)}) collective-permute-start(bf16[1024,256]{1,0:T(8,128)(2,1)S(1)} %get-tuple-element.219), channel_id=1, source_target_pairs={{0,4},{4,0},{8,12},{12,8},{16,20},{20,16},{24,28},{28,24},{1,5},{5... | collective-permute-start | bytes 1572872 | tf_op jit(solution)/shard_map/ppermute | solution.py:22
  85.2 12.4 %collective-permute-start.26 = (bf16[768,256]{1,0:T(8,128)(2,1)S(1)}, bf16[768,256]{1,0:T(8,128)(2,1)S(1)}, u32[]{:S(2)}, u32[]{:S(2)}) collective-permute-start(bf16[768,256]{1,0:T(8,128)(2,1)S(1)} %get-tuple-element.239), channel_id=1, source_target_pairs={{0,8},{4,12},{8,0},{12,4},{16,24},{20,28},{24,16},{28,20},{1,9},{5... | collective-permute-start | bytes 1179656 | tf_op jit(solution)/shard_map/ppermute | solution.py:22
  100.2 11.7 %collective-permute-start.29 = (bf16[400,256]{1,0:T(8,128)(2,1)S(1)}, bf16[400,256]{1,0:T(8,128)(2,1)S(1)}, u32[]{:S(2)}, u32[]{:S(2)}) collective-permute-start(bf16[400,256]{1,0:T(8,128)(2,1)S(1)} %get-tuple-element.248), channel_id=1, source_target_pairs={{0,8},{4,12},{8,0},{12,4},{16,24},{20,28},{24,16},{28,20},{1,9},{5... | collective-permute-start | bytes 614408 | tf_op jit(solution)/shard_map/ppermute | solution.py:22
  100.8 11.1 %collective-permute-start.30 = (bf16[384,256]{1,0:T(8,128)(2,1)S(1)}, bf16[384,256]{1,0:T(8,128)(2,1)S(1)}, u32[]{:S(2)}, u32[]{:S(2)}) collective-permute-start(bf16[384,256]{1,0:T(8,128)(2,1)S(1)} %get-tuple-element.251), channel_id=1, source_target_pairs={{0,16},{4,20},{8,24},{12,28},{16,0},{20,4},{24,8},{28,12},{1,17},{... | collective-permute-start | bytes 589832 | tf_op jit(solution)/shard_map/ppermute | solution.py:22
  103.6 10.9 %collective-permute-start.34 = (bf16[128,1024]{1,0:T(8,128)(2,1)S(1)}, bf16[128,1024]{1,0:T(8,128)(2,1)S(1)}, u32[]{:S(2)}, u32[]{:S(2)}) collective-permute-start(bf16[128,1024]{1,0:T(8,128)(2,1)S(1)} %get-tuple-element.258), channel_id=1, source_target_pairs={{0,2},{1,3},{2,0},{3,1},{4,6},{5,7},{6,4},{7,5},{8,10},{9,11},{10,... | collective-permute-start | bytes 786440 | tf_op jit(solution)/shard_map/ppermute | solution.py:22
  111.9 9.8 %collective-permute-start.31 = (bf16[400,256]{1,0:T(8,128)(2,1)S(1)}, bf16[400,256]{1,0:T(8,128)(2,1)S(1)}, u32[]{:S(2)}, u32[]{:S(2)}) collective-permute-start(bf16[400,256]{1,0:T(8,128)(2,1)S(1)} %shard_map.270.refs_0_), channel_id=1, source_target_pairs={{0,16},{4,20},{8,24},{12,28},{16,0},{20,4},{24,8},{28,12},{1,17},{... | collective-permute-start | bytes 614408 | tf_op jit(solution)/shard_map/ppermute | solution.py:22
  113.7 12.9 %collective-permute-start.37 = (bf16[64,2048]{1,0:T(8,128)(2,1)S(1)}, bf16[64,2048]{1,0:T(8,128)(2,1)S(1)}, u32[]{:S(2)}, u32[]{:S(2)}) collective-permute-start(bf16[64,2048]{1,0:T(8,128)(2,1)S(1)} %get-tuple-element.263), channel_id=1, source_target_pairs={{0,1},{1,0},{2,3},{3,2},{4,5},{5,4},{6,7},{7,6},{8,9},{9,8},{10,11... | collective-permute-start | bytes 786440 | tf_op jit(solution)/shard_map/ppermute | solution.py:22
  113.7 12.9 %collective-permute-start.38 = (bf16[64,2048]{1,0:T(8,128)(2,1)S(1)}, bf16[64,2048]{1,0:T(8,128)(2,1)S(1)}, u32[]{:S(2)}, u32[]{:S(2)}) collective-permute-start(bf16[64,2048]{1,0:T(8,128)(2,1)S(1)} %get-tuple-element.264), channel_id=1, source_target_pairs={{0,2},{1,3},{2,0},{3,1},{4,6},{5,7},{6,4},{7,5},{8,10},{9,11},{10,... | collective-permute-start | bytes 786440 | tf_op jit(solution)/shard_map/ppermute | solution.py:22
  114.5 13.2 %collective-permute-start.39 = (bf16[64,2048]{1,0:T(8,128)(2,1)S(1)}, bf16[64,2048]{1,0:T(8,128)(2,1)S(1)}, u32[]{:S(2)}, u32[]{:S(2)}) collective-permute-start(bf16[64,2048]{1,0:T(8,128)(2,1)S(1)} %get-tuple-element.265), channel_id=1, source_target_pairs={{0,3},{1,2},{2,1},{3,0},{4,7},{5,6},{6,5},{7,4},{8,11},{9,10},{10,... | collective-permute-start | bytes 786440 | tf_op jit(solution)/shard_map/ppermute | solution.py:22
  121.8 8.8 %collective-permute-start.36 = (bf16[384,256]{1,0:T(8,128)(2,1)S(1)}, bf16[384,256]{1,0:T(8,128)(2,1)S(1)}, u32[]{:S(2)}, u32[]{:S(2)}) collective-permute-start(bf16[384,256]{1,0:T(8,128)(2,1)S(1)} %shard_map.274), channel_id=1, source_target_pairs={{0,16},{4,20},{8,24},{12,28},{16,0},{20,4},{24,8},{28,12},{1,17},{... | collective-permute-start | bytes 589832 | tf_op jit(solution)/shard_map/ppermute | solution.py:22
  121.9 8.9 %collective-permute-start.35 = (bf16[384,256]{1,0:T(8,128)(2,1)S(1)}, bf16[384,256]{1,0:T(8,128)(2,1)S(1)}, u32[]{:S(2)}, u32[]{:S(2)}) collective-permute-start(bf16[384,256]{1,0:T(8,128)(2,1)S(1)} %get-tuple-element.260.refs_0_), channel_id=1, source_target_pairs={{0,8},{4,12},{8,0},{12,4},{16,24},{20,28},{24,16},{28,20},{1,9},{5... | collective-permute-start | bytes 589832 | tf_op jit(solution)/shard_map/ppermute | solution.py:22
  126.6 8.6 %collective-permute-start.42 = (f32[1,512]{1,0:T(1,128)S(1)}, f32[1,512]{1,0:T(1,128)S(1)}, u32[]{:S(2)}, u32[]{:S(2)}) collective-permute-start(f32[1,512]{1,0:T(1,128)S(1)} %bitcast.13), channel_id=1, source_target_pairs={{0,1},{1,0},{2,3},{3,2},{4,5},{5,4},{6,7},{7,6},{8,9},{9,8},{10,11... | collective-permute-start | bytes 6152 | tf_op jit(solution)/shard_map/ppermute | solution.py:22
  130.9 10.4 %collective-permute-start.41 = (bf16[768,256]{1,0:T(8,128)(2,1)S(1)}, bf16[768,256]{1,0:T(8,128)(2,1)S(1)}, u32[]{:S(2)}, u32[]{:S(2)}) collective-permute-start(bf16[768,256]{1,0:T(8,128)(2,1)S(1)} %pad_maximum_fusion.refs_2_), channel_id=1, source_target_pairs={{0,8},{4,12},{8,0},{12,4},{16,24},{20,28},{24,16},{28,20},{1,9},{5... | collective-permute-start | bytes 1179656 | tf_op jit(solution)/shard_map/ppermute | solution.py:22
  131.9 10.9 %collective-permute-start.40 = (bf16[768,256]{1,0:T(8,128)(2,1)S(1)}, bf16[768,256]{1,0:T(8,128)(2,1)S(1)}, u32[]{:S(2)}, u32[]{:S(2)}) collective-permute-start(bf16[768,256]{1,0:T(8,128)(2,1)S(1)} %shard_map.277.refs_0_), channel_id=1, source_target_pairs={{0,4},{4,0},{8,12},{12,8},{16,20},{20,16},{24,28},{28,24},{1,5},{5... | collective-permute-start | bytes 1179656 | tf_op jit(solution)/shard_map/ppermute | solution.py:22
  (27 other events, 113.5 us)
